TPU v7x, 32 devices: a whole 2x2x4 slice. The times are simulated.
32 devices in a mesh: blk: 2 (over x), grp: 16 (over z, y, core).
Axes of the slice: x: 2, y: 2, z: 4, core: 2. Of those that a mesh axis runs over, the one named last changes fastest.
Arguments:
- images: bfloat16 [512, 1152], P(('blk', 'grp')), may hold values from -6 to 6
- texts: bfloat16 [512, 1152], P(('blk', 'grp')), may hold values from -6 to 6
- scale: float32 [], replicated, may hold values from 8 to 16
- shift: float32 [], replicated, may hold values from -5 to -3
Outputs:
- image_loss: float32 [512], P(('blk', 'grp'))
- image_grad: float32 [512, 1152], P(('blk', 'grp'))
- text_grad: float32 [512, 1152], P(('blk', 'grp'))
All inputs are finite; a program needn't handle non-finite values.
Results may differ from a plain program's by a relative error of at most 0.0045.
Values may be sent and summed in bfloat16 or wider, within the bound.
No kernel may reach another device: no remote copies, remote signals or barrier semaphores. Data moves between devices by JAX's collectives and lax.ppermute only.
A program may use at most 64 MiB of HBM per device.

v0:
```python
import jax
import jax.numpy as jnp
from jax import lax
from jax.sharding import PartitionSpec as P


def passed_along(value, axis, steps):
    count = lax.axis_size(axis)
    pairs = [(source, (source + steps) % count) for source in range(count)]
    return lax.ppermute(value, axis, pairs)


def unit_rows(values):
    floats = values.astype(jnp.float32)
    norms = jnp.sqrt(jnp.sum(floats * floats, 1, keepdims=True) + 1e-06)
    return (floats / norms, norms)


def back_rows(grads, units, norms):
    return (grads - units * jnp.sum(units * grads, 1, keepdims=True)) / norms


def local(images, texts, scale, shift):
    rows = images.shape[0]
    image_unit, image_norm = unit_rows(images)
    text_unit, text_norm = unit_rows(texts)
    image_emb = image_unit.astype(jnp.bfloat16)
    text_emb = text_unit.astype(jnp.bfloat16)
    gathered = lax.all_gather(image_emb, "grp", axis=0, tiled=True)
    groups = lax.axis_size("grp")
    loops = lax.axis_size("blk")
    total = loops * groups * rows
    place = lax.axis_index("grp")
    image_ids = jnp.arange(groups * rows, dtype=jnp.int32)[:, None]
    column_ids = place * rows + jnp.arange(rows, dtype=jnp.int32)[None, :]
    own_label = (image_ids == column_ids).astype(jnp.float32)
    zero_label = jnp.zeros_like(own_label)
    text_now = text_emb
    loss_sum = jnp.zeros((groups * rows,), jnp.float32)
    carried = jnp.zeros((rows, images.shape[1]), jnp.float32)
    coefs = []
    seen = []
    for step in range(loops):
        label = own_label if step == 0 else zero_label
        logit = (
            scale
            * lax.dot_general(
                gathered, text_now, (((1,), (1,)), ((), ())), preferred_element_type=jnp.float32
            )
            + shift
        )
        loss = jnp.sum(jax.nn.softplus(logit * (1.0 - 2.0 * label)), 1) / total
        coef = ((jax.nn.sigmoid(logit) - label) * scale).astype(jnp.bfloat16)
        grad_text = lax.dot_general(
            coef, gathered, (((0,), (0,)), ((), ())), preferred_element_type=jnp.float32
        )
        loss, coef, grad_text = (loss, coef, grad_text)
        loss_sum = loss_sum + loss
        coefs.append(coef)
        seen.append(text_now)
        carried = passed_along(carried + grad_text, "blk", 1)
        if step + 1 < loops:
            text_now = passed_along(text_now, "blk", 1)
    left_side = jnp.concatenate(coefs, 1)
    right_side = jnp.concatenate(seen, 0)
    image_part = jnp.dot(left_side, right_side, preferred_element_type=jnp.float32)
    received = (
        lax.all_to_all(
            image_part.reshape(groups, rows, -1), "grp", split_axis=0, concat_axis=0, tiled=True
        ),
        lax.all_to_all(
            loss_sum.reshape(groups, rows), "grp", split_axis=0, concat_axis=0, tiled=True
        ),
    )
    image_sum = jnp.sum(received[0], 0)
    image_loss = jnp.sum(received[1], 0)
    image_grad = back_rows(image_sum, image_unit, image_norm)
    text_grad = back_rows(carried, text_unit, text_norm)
    return (image_loss, image_grad, text_grad)


def solution(mesh):
    in_specs = (P(("blk", "grp"), None), P(("blk", "grp"), None), P(), P())
    out_specs = (P(("blk", "grp")), P(("blk", "grp"), None), P(("blk", "grp"), None))
    return jax.shard_map(local, mesh=mesh, in_specs=in_specs, out_specs=out_specs, check_vma=False)
```

profile of v0, /device:TPU:13, one launch (start us, length us, event | category | flops | bytes accessed | tf_op | source)
XLA Modules:
  0.0 74.5 jit_solution(2222425694884841007)
XLA Ops:
  0.6 0.9 %fusion.3 = f32[16]{0:T(128)S(1)} fusion(bf16[16,1152]{1,0:T(8,128)(2,1)} %param.5), kind=kLoop, calls=%fused_computation.10 | loop fusion | flops 55280 | bytes 36928 | tf_op jit(solution)/shard_map/reduce_sum | solution.py:15
  1.5 0.9 %fusion.15 = bf16[16,1152]{1,0:T(8,128)(2,1)S(1)} fusion(f32[16]{0:T(128)S(1)} %add_sqrt_fusion, bf16[16,1152]{1,0:T(8,128)(2,1)} %param.5), kind=kLoop, calls=%fused_computation.35 | loop fusion | flops 55296 | bytes 73792 | tf_op jit(solution)/shard_map/convert_element_type | solution.py:28
  2.4 1.3 %collective-permute-start = (bf16[16,1152]{1,0:T(8,128)(2,1)S(1)}, bf16[16,1152]{1,0:T(8,128)(2,1)S(1)}, u32[]{:S(2)}, u32[]{:S(2)}) collective-permute-start(bf16[16,1152]{1,0:T(8,128)(2,1)S(1)} %fusion.15), channel_id=1, source_target_pairs={{0,16},{16,0},{1,17},{17,1},{2,18},{18,2},{3,19},{19,3},{4,20},{20... | collective-permute-start | bytes 110600 | tf_op jit(solution)/shard_map/ppermute | solution.py:10
  4.9 0.9 %fusion.2 = f32[16]{0:T(128)S(1)} fusion(bf16[16,1152]{1,0:T(8,128)(2,1)} %param.4), kind=kLoop, calls=%fused_computation.9 | loop fusion | flops 55280 | bytes 36928 | tf_op jit(solution)/shard_map/reduce_sum | solution.py:15
  5.8 0.9 %fusion.14 = bf16[16,1152]{1,0:T(8,128)(2,1)S(1)} fusion(f32[16]{0:T(128)S(1)} %add_sqrt_fusion.1, bf16[16,1152]{1,0:T(8,128)(2,1)} %param.4), kind=kLoop, calls=%fused_computation.34 | loop fusion | flops 55296 | bytes 73792 | tf_op jit(solution)/shard_map/convert_element_type | solution.py:27
  6.7 17.5 %all_gather.3 = bf16[256,1152]{1,0:T(8,128)(2,1)S(1)} all-gather(bf16[16,1152]{1,0:T(8,128)(2,1)S(1)} %fusion.14), channel_id=1, replica_groups=mesh['blk'=2,'grp'=16] {'grp'}, dimensions={0}, use_global_device_ids=true | all-gather | bytes 626688 | tf_op jit(solution)/shard_map/all_gather | solution.py:29
  24.2 0.3 multiply_convert_fusion.1
  24.5 0.0 collective-permute-done
  24.6 0.3 multiply_convert_fusion
  24.9 0.7 add.78
  25.6 10.2 %all-to-all-start = ((f32[16,1,16]{2,1,0:T(1,128)}), f32[16,1,16]{2,1,0:T(1,128)S(1)}, u32[]{:S(2)}, u32[]{:S(2)}) async-start(f32[16,1,16]{2,1,0:T(1,128)} %add.78), calls=%async_computation | async-start | bytes 16384 | tf_op jit(solution)/shard_map/all_to_all | solution.py:71
  35.7 1.3 %fusion.4 = f32[256,1152]{1,0:T(8,128)} fusion(bf16[16,1152]{1,0:T(8,128)(2,1)S(1)} %collective-permute-done, bf16[16,1152]{1,0:T(8,128)(2,1)S(1)} %fusion.15, bf16[256,16]{0,1:T(8,128)(2,1)S(1)} %get-tuple-element.5, bf16[256,16]{0,1:T(8,128)(2,1)S(1)} %get-tuple-element.3), kind=kOutput, calls=%fused_computation.11 | convolution fusion | flops 19054592 | bytes 1269760 | tf_op jit(solution)/shard_map/dot_general | solution.py:66
  37.1 2.4 %all-to-all-done = f32[16,1,16]{2,1,0:T(1,128)S(1)} async-done(((f32[16,1,16]{2,1,0:T(1,128)}), f32[16,1,16]{2,1,0:T(1,128)S(1)}, u32[]{:S(2)}, u32[]{:S(2)}) %all-to-all-start) | async-done | bytes 1056 | tf_op jit(solution)/shard_map/all_to_all | solution.py:71
  39.5 6.2 %all-to-all-start.1 = ((f32[16,16,1152]{2,1,0:T(8,128)}), f32[16,16,1152]{2,1,0:T(8,128)S(1)}, u32[]{:S(2)}, u32[]{:S(2)}) async-start(f32[16,16,1152]{2,1,0:T(8,128)} %bitcast.1), calls=%async_computation.1 | async-start | bytes 2359296 | tf_op jit(solution)/shard_map/all_to_all | solution.py:68
  45.7 0.0 copy-start
  45.7 0.2 fusion.16
  45.9 0.0 copy-start.1
  45.9 0.3 collective-permute-start.1
  46.3 3.2 %collective-permute-done.1 = f32[16,1152]{1,0:T(8,128)S(1)} collective-permute-done((f32[16,1152]{1,0:T(8,128)S(1)}, f32[16,1152]{1,0:T(8,128)S(1)}, u32[]{:S(2)}, u32[]{:S(2)}) %collective-permute-start.1) | collective-permute-done | bytes 73760 | tf_op jit(solution)/shard_map/ppermute | solution.py:10
  49.5 0.2 convolution_add_fusion
  49.7 0.3 collective-permute-start.2
  50.0 0.5 reduce_sum.76
  50.6 2.7 %collective-permute-done.2 = f32[16,1152]{1,0:T(8,128)S(1)} collective-permute-done((f32[16,1152]{1,0:T(8,128)S(1)}, f32[16,1152]{1,0:T(8,128)S(1)}, u32[]{:S(2)}, u32[]{:S(2)}) %collective-permute-start.2) | collective-permute-done | bytes 73760 | tf_op jit(solution)/shard_map/ppermute | solution.py:10
  53.3 0.0 copy-done
  53.3 0.2 multiply_reduce_fusion
  53.5 0.7 subtract_divide_fusion
  54.2 19.3 %all-to-all-done.1 = f32[16,16,1152]{2,1,0:T(8,128)S(1)} async-done(((f32[16,16,1152]{2,1,0:T(8,128)}), f32[16,16,1152]{2,1,0:T(8,128)S(1)}, u32[]{:S(2)}, u32[]{:S(2)}) %all-to-all-start.1) | async-done | bytes 1179680 | tf_op jit(solution)/shard_map/all_to_all | solution.py:68
  73.5 0.1 reduce_sum.77
  73.6 0.0 copy-done.1
  73.6 0.2 multiply_reduce_fusion.1
  73.8 0.7 subtract_divide_fusion.1
  (4 shorter events, 0.0 us)
Async XLA Ops:
  2.4 22.2 %collective-permute-start = (bf16[16,1152]{1,0:T(8,128)(2,1)S(1)}, bf16[16,1152]{1,0:T(8,128)(2,1)S(1)}, u32[]{:S(2)}, u32[]{:S(2)}) collective-permute-start(bf16[16,1152]{1,0:T(8,128)(2,1)S(1)} %fusion.15), channel_id=1, source_target_pairs={{0,16},{16,0},{1,17},{17,1},{2,18},{18,2},{3,19},{19,3},{4,20},{20... | collective-permute-start | bytes 110600 | tf_op jit(solution)/shard_map/ppermute | solution.py:10
  25.6 13.9 %all-to-all-start = ((f32[16,1,16]{2,1,0:T(1,128)}), f32[16,1,16]{2,1,0:T(1,128)S(1)}, u32[]{:S(2)}, u32[]{:S(2)}) async-start(f32[16,1,16]{2,1,0:T(1,128)} %add.78), calls=%async_computation | async-start | bytes 16384 | tf_op jit(solution)/shard_map/all_to_all | solution.py:71
  39.5 34.0 %all-to-all-start.1 = ((f32[16,16,1152]{2,1,0:T(8,128)}), f32[16,16,1152]{2,1,0:T(8,128)S(1)}, u32[]{:S(2)}, u32[]{:S(2)}) async-start(f32[16,16,1152]{2,1,0:T(8,128)} %bitcast.1), calls=%async_computation.1 | async-start | bytes 2359296 | tf_op jit(solution)/shard_map/all_to_all | solution.py:68
  45.7 7.5 %copy-start = (bf16[16,1152]{1,0:T(8,128)(2,1)S(1)}, bf16[16,1152]{1,0:T(8,128)(2,1)}, u32[]{:S(2)}) copy-start(bf16[16,1152]{1,0:T(8,128)(2,1)} %param.5) | copy-start | bytes 110596
  45.9 27.6 %copy-start.1 = (bf16[16,1152]{1,0:T(8,128)(2,1)S(1)}, bf16[16,1152]{1,0:T(8,128)(2,1)}, u32[]{:S(2)}) copy-start(bf16[16,1152]{1,0:T(8,128)(2,1)} %param.4) | copy-start | bytes 110596
  45.9 3.6 %collective-permute-start.1 = (f32[16,1152]{1,0:T(8,128)S(1)}, f32[16,1152]{1,0:T(8,128)S(1)}, u32[]{:S(2)}, u32[]{:S(2)}) collective-permute-start(f32[16,1152]{1,0:T(8,128)S(1)} %fusion.16), channel_id=1, source_target_pairs={{0,16},{16,0},{1,17},{17,1},{2,18},{18,2},{3,19},{19,3},{4,20},{20... | collective-permute-start | bytes 221192 | tf_op jit(solution)/shard_map/ppermute | solution.py:10
  49.7 3.6 %collective-permute-start.2 = (f32[16,1152]{1,0:T(8,128)S(1)}, f32[16,1152]{1,0:T(8,128)S(1)}, u32[]{:S(2)}, u32[]{:S(2)}) collective-permute-start(f32[16,1152]{1,0:T(8,128)S(1)} %convolution_add_fusion), channel_id=1, source_target_pairs={{0,16},{16,0},{1,17},{17,1},{2,18},{18,2},{3,19},{19,3},{4,20},{20... | collective-permute-start | bytes 221192 | tf_op jit(solution)/shard_map/ppermute | solution.py:10
where the time goes:
time: 75 us; the launch traced here: 74.5 us
  waiting for transfers between devices  27.7 us (37%)
  starting transfers between devices  18.3 us (24%)
  blocking collectives  17.5 us (23%)
  other arithmetic  5.95 us (8%)
  matrix products  2.37 us (3%)
  between operations  1.99 us (3%)
    all_to_all x1, waiting for transfers between devices, local(): lax.all_to_all(image_part.reshape(groups, rows, -1), 'grp', split_axis=0,...  19.3 us
    all_gather x1, blocking collectives, local(): gathered = lax.all_gather(image_emb, 'grp', axis=0, tiled=True)  17.5 us
    all_to_all x1, starting transfers between devices, local(): lax.all_to_all(loss_sum.reshape(groups, rows), 'grp', split_axis=0, conca...  10.2 us
    all_to_all x1, starting transfers between devices, local(): lax.all_to_all(image_part.reshape(groups, rows, -1), 'grp', split_axis=0,...  6.23 us
    ppermute x3, waiting for transfers between devices, passed_along(): return lax.ppermute(value, axis, pairs)  5.96 us
    all_to_all x1, waiting for transfers between devices, local(): lax.all_to_all(loss_sum.reshape(groups, rows), 'grp', split_axis=0, conca...  2.43 us
    ppermute x3, starting transfers between devices, passed_along(): return lax.ppermute(value, axis, pairs)  1.89 us
    reduce_sum x2, other arithmetic, unit_rows(): norms = jnp.sqrt(jnp.sum(floats * floats, 1, keepdims=True) + 1e-06)  1.78 us
  transfers between devices with their start and end apart: 5, of which 4 were waited for; matrix products, arithmetic and copies ran while one was open for 7% of the time, Pallas kernels for 0%

commit v1 on v0

v1 whole, which is shorter than its diff:
```python
import functools

import jax
import jax.numpy as jnp
from jax import lax
from jax.experimental import pallas as pl
from jax.experimental.pallas import tpu as pltpu
from jax.sharding import PartitionSpec as P

AXES = ("blk", "grp")
LANES = 128
VMEM_BYTES = 24 * 1024 * 1024


def spread(value, bits):
    return sum(bit for place, bit in enumerate(bits) if value >> place & 1)


def plan(blocks, groups):
    bits = [1 << place for place in range((blocks * groups).bit_length() - 1)][1:]
    half = len(bits) // 2
    top = [bit for bit in bits if bit >= groups]
    low = [bit for bit in bits if bit < groups]
    need = half - len(top)
    image_bits = low[:need] + top
    text_bits = low[need:]
    order = sorted(
        range(1, 1 << half), key=lambda k: -bin(k).count("1")
    )
    return [(spread(k, image_bits), spread(k, text_bits)) for k in order]


def permuted(value, devices, image_step, text_step):
    pairs = [(d, d ^ (text_step if d & 1 else image_step)) for d in range(devices)]
    return lax.ppermute(value, AXES, pairs)


def first_core():
    return lax.axis_index("grp") % 2 == 0


def units(values):
    floats = values.astype(jnp.float32)
    norms = jnp.sqrt(jnp.sum(floats * floats, 1, keepdims=True) + 1e-06)
    return floats / norms, norms


def embed_kernel(images, texts, keep, send):
    image_emb = units(images[...])[0].astype(jnp.bfloat16)
    text_emb = units(texts[...])[0].astype(jnp.bfloat16)
    first = first_core()

    @pl.when(first)
    def _():
        keep[...] = image_emb
        send[...] = text_emb

    @pl.when(jnp.logical_not(first))
    def _():
        keep[...] = text_emb
        send[...] = image_emb


def tile_kernel(rows, total, scale_ref, shift_ref, mine, other, *outs):
    scale = scale_ref[0]
    shift = shift_ref[0]
    own = mine[...]
    far = other[...]
    count = own.shape[0]
    size = 2 * rows
    nt = (((1,), (1,)), ((), ()))
    row = lax.broadcasted_iota(jnp.int32, (count, count), 0)
    column = lax.broadcasted_iota(jnp.int32, (count, count), 1)
    hit = jnp.logical_and(row == column, row < size)
    label = hit.astype(jnp.float32)
    logit = scale * lax.dot_general(own, far, nt, preferred_element_type=jnp.float32) + shift
    coef = ((jax.nn.sigmoid(logit) - label) * scale).astype(jnp.bfloat16)
    grad = jnp.dot(coef, far, preferred_element_type=jnp.float32)
    turned = scale * lax.dot_general(far, own, nt, preferred_element_type=jnp.float32) + shift
    signed = turned * (1.0 - 2.0 * label)
    soft = jnp.maximum(signed, 0.0) + jnp.log1p(jnp.exp(-jnp.abs(signed)))
    loss = jnp.sum(soft, 0, keepdims=True) / total
    chunks = own.shape[1] // LANES
    for slot, out in enumerate(outs):
        for core in range(2):
            top = slot * size + core * rows
            for chunk in range(chunks):
                at = (core * chunks + chunk) * rows
                out[at : at + rows, :] = grad[top : top + rows, chunk * LANES : (chunk + 1) * LANES]
        lane = slot * size
        part = loss[:, lane // LANES * LANES : lane // LANES * LANES + LANES]
        part = jnp.broadcast_to(part, (8, LANES))
        if lane % LANES:
            part = pltpu.roll(part, LANES - lane % LANES, 1)
        out[2 * chunks * rows :, :] = part


def finish_kernel(images, texts, kept, came, loss_out, image_out, text_out):
    rows, width = images.shape
    chunks = width // LANES
    first = first_core()

    def back(raw, grads):
        unit, norm = units(raw[...])
        grad = jnp.concatenate(
            [grads[chunk * rows : (chunk + 1) * rows, :] for chunk in range(chunks)], 1
        )
        return (grad - unit * jnp.sum(unit * grad, 1, keepdims=True)) / norm

    @pl.when(first)
    def _():
        loss_out[...] = kept[chunks * rows : chunks * rows + 1, :]
        image_out[...] = back(images, kept)
        text_out[...] = back(texts, came)

    @pl.when(jnp.logical_not(first))
    def _():
        loss_out[...] = pltpu.roll(came[chunks * rows :, :], LANES - rows, 1)[:1]
        image_out[...] = back(images, came)
        text_out[...] = back(texts, kept)


def vmem(count):
    return [pl.BlockSpec(memory_space=pltpu.VMEM)] * count


def local(images, texts, scale, shift, blocks, groups):
    rows, width = images.shape
    devices = blocks * groups
    params = pltpu.CompilerParams(vmem_limit_bytes=VMEM_BYTES)
    steps = plan(blocks, groups)
    chunks = width // LANES
    first = first_core()
    piece = jax.ShapeDtypeStruct((rows, width), jnp.bfloat16)
    keep, send = pl.pallas_call(
        embed_kernel,
        out_shape=(piece, piece),
        in_specs=vmem(2),
        out_specs=tuple(vmem(2)),
        compiler_params=params,
        name="embed",
    )(images, texts)
    got = permuted(send, devices, 1, 1)
    chip = jnp.where(first, jnp.concatenate([keep, got], 0), jnp.concatenate([got, keep], 0))
    gathered = [permuted(chip, devices, a, b) for a, b in reversed(steps)][::-1]
    mine = jnp.concatenate([chip] + gathered, 0)
    other = permuted(mine, devices, 1, 1)
    message = jax.ShapeDtypeStruct((2 * chunks * rows + 8, LANES), jnp.float32)
    parts = pl.pallas_call(
        functools.partial(tile_kernel, rows, devices * rows),
        out_shape=[message] * (len(steps) + 1),
        in_specs=[pl.BlockSpec(memory_space=pltpu.SMEM)] * 2 + vmem(2),
        out_specs=vmem(len(steps) + 1),
        compiler_params=params,
        name="tile",
    )(scale.reshape(1), shift.reshape(1), mine, other)
    arrived = [permuted(part, devices, a, b) for part, (a, b) in zip(parts[1:], steps)]
    whole = parts[0]
    for part in arrived:
        whole = whole + part
    half = chunks * rows
    upper, lower, tail = whole[:half], whole[half : 2 * half], whole[2 * half :]
    kept = jnp.concatenate([jnp.where(first, upper, lower), tail], 0)
    leaving = jnp.concatenate([jnp.where(first, lower, upper), tail], 0)
    came = permuted(leaving, devices, 1, 1)
    loss, image_grad, text_grad = pl.pallas_call(
        finish_kernel,
        out_shape=(
            jax.ShapeDtypeStruct((1, LANES), jnp.float32),
            jax.ShapeDtypeStruct((rows, width), jnp.float32),
            jax.ShapeDtypeStruct((rows, width), jnp.float32),
        ),
        in_specs=vmem(4),
        out_specs=tuple(vmem(3)),
        compiler_params=params,
        name="finish",
    )(images, texts, kept, came)
    return loss[0, :rows], image_grad, text_grad


def solution(mesh):
    in_specs = (P(AXES, None), P(AXES, None), P(), P())
    out_specs = (P(AXES), P(AXES, None), P(AXES, None))
    step = functools.partial(local, blocks=mesh.shape["blk"], groups=mesh.shape["grp"])
    return jax.shard_map(step, mesh=mesh, in_specs=in_specs, out_specs=out_specs, check_vma=False)
```

time: 75 us -> 28.7 us (0.38)
  the two profiles are of different devices: /device:TPU:13 before, /device:TPU:0 now
where the time goes in v1:
time: 28.7 us; the launch traced here: 28.5 us
  waiting for transfers between devices  11.7 us (41%)
  starting transfers between devices  10.9 us (38%)
  local copies, waits for them, and re-layouts  2.06 us (7%)
  between operations  2 us (7%)
  Pallas kernels  1.76 us (6%)
    ppermute x9, waiting for transfers between devices, permuted(): return lax.ppermute(value, AXES, pairs)  11.7 us
    ppermute x9, starting transfers between devices, permuted(): return lax.ppermute(value, AXES, pairs)  10.9 us
    unnamed x8, local copies, waits for them, and re-layouts  1.54 us
    pallas_call x1, Pallas kernels, local(): pl.pallas_call(finish_kernel, out_shape=(jax.ShapeDtypeStruct((1, LANES),...  0.87 us
    pallas_call x1, Pallas kernels, local(): pl.pallas_call(functools.partial(tile_kernel, rows, devices * rows), out_...  0.77 us
  transfers between devices with their start and end apart: 9, of which 8 were waited for; matrix products, arithmetic and copies ran while one was open for 0% of the time, Pallas kernels for 0%

profile of v1, /device:TPU:0, one launch (start us, length us, event | category | flops | bytes accessed | tf_op | source)
XLA Modules:
  0.0 28.5 jit_solution(11276012912167979075)
XLA Ops:
  0.6 0.0 copy-start
  0.6 0.8 %copy-done = bf16[16,1152]{1,0:T(8,128)(2,1)S(1)} copy-done((bf16[16,1152]{1,0:T(8,128)(2,1)S(1)}, bf16[16,1152]{1,0:T(8,128)(2,1)}, u32[]{:S(2)}) %copy-start) | copy-done | bytes 36888
  1.4 0.0 copy-start.2
  1.4 0.8 %copy-done.2 = bf16[16,1152]{1,0:T(8,128)(2,1)S(1)} copy-done((bf16[16,1152]{1,0:T(8,128)(2,1)S(1)}, bf16[16,1152]{1,0:T(8,128)(2,1)}, u32[]{:S(2)}) %copy-start.2) | copy-done | bytes 36888
  2.2 0.1 embed.1
  2.3 0.5 %collective-permute-start = (bf16[16,1152]{1,0:T(8,128)(2,1)S(1)}, bf16[16,1152]{1,0:T(8,128)(2,1)S(1)}, u32[]{:S(2)}, u32[]{:S(2)}) collective-permute-start(bf16[16,1152]{1,0:T(8,128)(2,1)S(1)} %get-tuple-element.13), channel_id=1, source_target_pairs={{0,1},{1,0},{2,3},{3,2},{4,5},{5,4},{6,7},{7,6},{8,9},{9,8},{10,11... | collective-permute-start | bytes 110600 | tf_op jit(solution)/shard_map/ppermute | solution.py:35
  2.8 0.9 %collective-permute-done = bf16[16,1152]{1,0:T(8,128)(2,1)S(1)} collective-permute-done((bf16[16,1152]{1,0:T(8,128)(2,1)S(1)}, bf16[16,1152]{1,0:T(8,128)(2,1)S(1)}, u32[]{:S(2)}, u32[]{:S(2)}) %collective-permute-start) | collective-permute-done | bytes 36896 | tf_op jit(solution)/shard_map/ppermute | solution.py:35
  3.7 2.9 %collective-permute-start.3 = (bf16[32,1152]{1,0:T(8,128)(2,1)S(1)}, bf16[32,1152]{1,0:T(8,128)(2,1)S(1)}, u32[]{:S(2)}, u32[]{:S(2)}) collective-permute-start(bf16[32,1152]{1,0:T(8,128)(2,1)S(1)} %maximum_select_fusion), channel_id=1, source_target_pairs={{0,16},{1,9},{2,18},{3,11},{4,20},{5,13},{6,22},{7,15},{8,24},{9,1... | collective-permute-start | bytes 221192 | tf_op jit(solution)/shard_map/ppermute | solution.py:35
  6.6 1.5 %collective-permute-start.2 = (bf16[32,1152]{1,0:T(8,128)(2,1)S(1)}, bf16[32,1152]{1,0:T(8,128)(2,1)S(1)}, u32[]{:S(2)}, u32[]{:S(2)}) collective-permute-start(bf16[32,1152]{1,0:T(8,128)(2,1)S(1)} %maximum_select_fusion), channel_id=1, source_target_pairs={{0,2},{1,5},{2,0},{3,7},{4,6},{5,1},{6,4},{7,3},{8,10},{9,13},{10,... | collective-permute-start | bytes 221192 | tf_op jit(solution)/shard_map/ppermute | solution.py:35
  8.1 0.0 collective-permute-start.1
  8.1 0.8 %collective-permute-done.3 = bf16[32,1152]{1,0:T(8,128)(2,1)S(1)} collective-permute-done((bf16[32,1152]{1,0:T(8,128)(2,1)S(1)}, bf16[32,1152]{1,0:T(8,128)(2,1)S(1)}, u32[]{:S(2)}, u32[]{:S(2)}) %collective-permute-start.3) | collective-permute-done | bytes 73760 | tf_op jit(solution)/shard_map/ppermute | solution.py:35
  8.9 2.0 %collective-permute-done.2 = bf16[32,1152]{1,0:T(8,128)(2,1)S(1)} collective-permute-done((bf16[32,1152]{1,0:T(8,128)(2,1)S(1)}, bf16[32,1152]{1,0:T(8,128)(2,1)S(1)}, u32[]{:S(2)}, u32[]{:S(2)}) %collective-permute-start.2) | collective-permute-done | bytes 73760 | tf_op jit(solution)/shard_map/ppermute | solution.py:35
  10.9 2.4 %collective-permute-done.1 = bf16[32,1152]{1,0:T(8,128)(2,1)S(1)} collective-permute-done((bf16[32,1152]{1,0:T(8,128)(2,1)S(1)}, bf16[32,1152]{1,0:T(8,128)(2,1)S(1)}, u32[]{:S(2)}, u32[]{:S(2)}) %collective-permute-start.1) | collective-permute-done | bytes 73760 | tf_op jit(solution)/shard_map/ppermute | solution.py:35
  13.4 0.6 %collective-permute-start.4 = (bf16[128,1152]{1,0:T(8,128)(2,1)S(1)}, bf16[128,1152]{1,0:T(8,128)(2,1)S(1)}, u32[]{:S(2)}, u32[]{:S(2)}) collective-permute-start(bf16[128,1152]{1,0:T(8,128)(2,1)S(1)} %pad_maximum_fusion.mine), channel_id=1, source_target_pairs={{0,1},{1,0},{2,3},{3,2},{4,5},{5,4},{6,7},{7,6},{8,9},{9,8},{10,11... | collective-permute-start | bytes 884744 | tf_op jit(solution)/shard_map/ppermute | solution.py:35
  15.3 0.0 collective-permute-done.4.other
  15.3 0.8 %tile.1 = (f32[296,128]{1,0:T(8,128)S(1)}, f32[296,128]{1,0:T(8,128)S(1)}, f32[296,128]{1,0:T(8,128)S(1)}, f32[296,128]{1,0:T(8,128)S(1)}) custom-call(f32[1]{0:T(128)} %bitcast.4.scale_ref, f32[1]{0:T(128)} %bitcast.5.shift_ref, bf16[128,1152]{1,0:T(8,128)(2,1)S(1)} %pad_maximum_fusion.mine, bf16[128,1152]{1,0:T(8,128)(2,1)S(1)} %collective-permute-done.4.other), custom_call_target="tpu_custom_call" | custom-call | tf_op jit(solution)/shard_map/tile/pallas_call | solution.py:149
  16.1 2.4 %collective-permute-start.5 = (f32[296,128]{1,0:T(8,128)S(1)}, f32[296,128]{1,0:T(8,128)S(1)}, u32[]{:S(2)}, u32[]{:S(2)}) collective-permute-start(f32[296,128]{1,0:T(8,128)S(1)} %get-tuple-element.15), channel_id=1, source_target_pairs={{0,18},{1,13},{2,16},{3,15},{4,22},{5,9},{6,20},{7,11},{8,26},{9,5... | collective-permute-start | bytes 454664 | tf_op jit(solution)/shard_map/ppermute | solution.py:35
  18.5 0.5 %collective-permute-start.6 = (f32[296,128]{1,0:T(8,128)S(1)}, f32[296,128]{1,0:T(8,128)S(1)}, u32[]{:S(2)}, u32[]{:S(2)}) collective-permute-start(f32[296,128]{1,0:T(8,128)S(1)} %get-tuple-element.16), channel_id=1, source_target_pairs={{0,2},{1,5},{2,0},{3,7},{4,6},{5,1},{6,4},{7,3},{8,10},{9,13},{10,... | collective-permute-start | bytes 454664 | tf_op jit(solution)/shard_map/ppermute | solution.py:35
  19.0 0.5 %collective-permute-start.7 = (f32[296,128]{1,0:T(8,128)S(1)}, f32[296,128]{1,0:T(8,128)S(1)}, u32[]{:S(2)}, u32[]{:S(2)}) collective-permute-start(f32[296,128]{1,0:T(8,128)S(1)} %get-tuple-element.17), channel_id=1, source_target_pairs={{0,16},{1,9},{2,18},{3,11},{4,20},{5,13},{6,22},{7,15},{8,24},{9,1... | collective-permute-start | bytes 454664 | tf_op jit(solution)/shard_map/ppermute | solution.py:35
  19.5 2.6 %collective-permute-done.5 = f32[296,128]{1,0:T(8,128)S(1)} collective-permute-done((f32[296,128]{1,0:T(8,128)S(1)}, f32[296,128]{1,0:T(8,128)S(1)}, u32[]{:S(2)}, u32[]{:S(2)}) %collective-permute-start.5) | collective-permute-done | bytes 151584 | tf_op jit(solution)/shard_map/ppermute | solution.py:35
  22.1 1.6 %collective-permute-done.6 = f32[296,128]{1,0:T(8,128)S(1)} collective-permute-done((f32[296,128]{1,0:T(8,128)S(1)}, f32[296,128]{1,0:T(8,128)S(1)}, u32[]{:S(2)}, u32[]{:S(2)}) %collective-permute-start.6) | collective-permute-done | bytes 151584 | tf_op jit(solution)/shard_map/ppermute | solution.py:35
  23.8 0.4 %collective-permute-done.7 = f32[296,128]{1,0:T(8,128)S(1)} collective-permute-done((f32[296,128]{1,0:T(8,128)S(1)}, f32[296,128]{1,0:T(8,128)S(1)}, u32[]{:S(2)}, u32[]{:S(2)}) %collective-permute-start.7) | collective-permute-done | bytes 151584 | tf_op jit(solution)/shard_map/ppermute | solution.py:35
  24.2 0.1 add_add_fusion
  24.3 0.0 copy-start.1
  24.3 0.0 copy-start.3
  24.3 1.8 %collective-permute-start.8 = (f32[152,128]{1,0:T(8,128)S(1)}, f32[152,128]{1,0:T(8,128)S(1)}, u32[]{:S(2)}, u32[]{:S(2)}) collective-permute-start(f32[152,128]{1,0:T(8,128)S(1)} %get-tuple-element.23), channel_id=1, source_target_pairs={{0,1},{1,0},{2,3},{3,2},{4,5},{5,4},{6,7},{7,6},{8,9},{9,8},{10,11... | collective-permute-start | bytes 233480 | tf_op jit(solution)/shard_map/ppermute | solution.py:35
  26.2 0.9 %collective-permute-done.8.came = f32[152,128]{1,0:T(8,128)S(1)} collective-permute-done((f32[152,128]{1,0:T(8,128)S(1)}, f32[152,128]{1,0:T(8,128)S(1)}, u32[]{:S(2)}, u32[]{:S(2)}) %collective-permute-start.8) | collective-permute-done | bytes 77856 | tf_op jit(solution)/shard_map/ppermute | solution.py:35
  27.1 0.0 copy-done.1
  27.1 0.0 copy-done.3
  27.1 0.9 %finish.1 = (f32[1,128]{1,0:T(1,128)S(1)}, f32[16,1152]{1,0:T(8,128)}, f32[16,1152]{1,0:T(8,128)}) custom-call(bf16[16,1152]{1,0:T(8,128)(2,1)S(1)} %copy-done.1, bf16[16,1152]{1,0:T(8,128)(2,1)S(1)} %copy-done.3, f32[152,128]{1,0:T(8,128)S(1)} %get-tuple-element.24.kept, f32[152,128]{1,0:T(8,128)S(1)} %collective-permute-done.8.came), custom_call_target="tpu_custom_call" | custom-call | tf_op jit(solution)/shard_map/finish/pallas_call | solution.py:166
  28.0 0.5 %slice_bitcast_fusion = f32[16]{0:T(128)} fusion(f32[1,128]{1,0:T(1,128)S(1)} %get-tuple-element.18), kind=kLoop, calls=%fused_computation.7 | loop fusion | bytes 128 | tf_op jit(solution)/shard_map/squeeze | solution.py:178
  (5 shorter events, 0.1 us)
Async XLA Ops:
  0.6 0.8 %copy-start = (bf16[16,1152]{1,0:T(8,128)(2,1)S(1)}, bf16[16,1152]{1,0:T(8,128)(2,1)}, u32[]{:S(2)}) copy-start(bf16[16,1152]{1,0:T(8,128)(2,1)} %images.3) | copy-start | bytes 110596
  1.4 0.8 %copy-start.2 = (bf16[16,1152]{1,0:T(8,128)(2,1)S(1)}, bf16[16,1152]{1,0:T(8,128)(2,1)}, u32[]{:S(2)}) copy-start(bf16[16,1152]{1,0:T(8,128)(2,1)} %texts.3) | copy-start | bytes 110596
  2.3 1.4 %collective-permute-start = (bf16[16,1152]{1,0:T(8,128)(2,1)S(1)}, bf16[16,1152]{1,0:T(8,128)(2,1)S(1)}, u32[]{:S(2)}, u32[]{:S(2)}) collective-permute-start(bf16[16,1152]{1,0:T(8,128)(2,1)S(1)} %get-tuple-element.13), channel_id=1, source_target_pairs={{0,1},{1,0},{2,3},{3,2},{4,5},{5,4},{6,7},{7,6},{8,9},{9,8},{10,11... | collective-permute-start | bytes 110600 | tf_op jit(solution)/shard_map/ppermute | solution.py:35
  3.7 5.2 %collective-permute-start.3 = (bf16[32,1152]{1,0:T(8,128)(2,1)S(1)}, bf16[32,1152]{1,0:T(8,128)(2,1)S(1)}, u32[]{:S(2)}, u32[]{:S(2)}) collective-permute-start(bf16[32,1152]{1,0:T(8,128)(2,1)S(1)} %maximum_select_fusion), channel_id=1, source_target_pairs={{0,16},{1,9},{2,18},{3,11},{4,20},{5,13},{6,22},{7,15},{8,24},{9,1... | collective-permute-start | bytes 221192 | tf_op jit(solution)/shard_map/ppermute | solution.py:35
  6.6 4.4 %collective-permute-start.2 = (bf16[32,1152]{1,0:T(8,128)(2,1)S(1)}, bf16[32,1152]{1,0:T(8,128)(2,1)S(1)}, u32[]{:S(2)}, u32[]{:S(2)}) collective-permute-start(bf16[32,1152]{1,0:T(8,128)(2,1)S(1)} %maximum_select_fusion), channel_id=1, source_target_pairs={{0,2},{1,5},{2,0},{3,7},{4,6},{5,1},{6,4},{7,3},{8,10},{9,13},{10,... | collective-permute-start | bytes 221192 | tf_op jit(solution)/shard_map/ppermute | solution.py:35
  8.1 5.3 %collective-permute-start.1 = (bf16[32,1152]{1,0:T(8,128)(2,1)S(1)}, bf16[32,1152]{1,0:T(8,128)(2,1)S(1)}, u32[]{:S(2)}, u32[]{:S(2)}) collective-permute-start(bf16[32,1152]{1,0:T(8,128)(2,1)S(1)} %maximum_select_fusion), channel_id=1, source_target_pairs={{0,18},{1,13},{2,16},{3,15},{4,22},{5,9},{6,20},{7,11},{8,26},{9,5... | collective-permute-start | bytes 221192 | tf_op jit(solution)/shard_map/ppermute | solution.py:35
  13.4 1.9 %collective-permute-start.4 = (bf16[128,1152]{1,0:T(8,128)(2,1)S(1)}, bf16[128,1152]{1,0:T(8,128)(2,1)S(1)}, u32[]{:S(2)}, u32[]{:S(2)}) collective-permute-start(bf16[128,1152]{1,0:T(8,128)(2,1)S(1)} %pad_maximum_fusion.mine), channel_id=1, source_target_pairs={{0,1},{1,0},{2,3},{3,2},{4,5},{5,4},{6,7},{7,6},{8,9},{9,8},{10,11... | collective-permute-start | bytes 884744 | tf_op jit(solution)/shard_map/ppermute | solution.py:35
  16.1 6.1 %collective-permute-start.5 = (f32[296,128]{1,0:T(8,128)S(1)}, f32[296,128]{1,0:T(8,128)S(1)}, u32[]{:S(2)}, u32[]{:S(2)}) collective-permute-start(f32[296,128]{1,0:T(8,128)S(1)} %get-tuple-element.15), channel_id=1, source_target_pairs={{0,18},{1,13},{2,16},{3,15},{4,22},{5,9},{6,20},{7,11},{8,26},{9,5... | collective-permute-start | bytes 454664 | tf_op jit(solution)/shard_map/ppermute | solution.py:35
  18.5 5.3 %collective-permute-start.6 = (f32[296,128]{1,0:T(8,128)S(1)}, f32[296,128]{1,0:T(8,128)S(1)}, u32[]{:S(2)}, u32[]{:S(2)}) collective-permute-start(f32[296,128]{1,0:T(8,128)S(1)} %get-tuple-element.16), channel_id=1, source_target_pairs={{0,2},{1,5},{2,0},{3,7},{4,6},{5,1},{6,4},{7,3},{8,10},{9,13},{10,... | collective-permute-start | bytes 454664 | tf_op jit(solution)/shard_map/ppermute | solution.py:35
  19.0 5.2 %collective-permute-start.7 = (f32[296,128]{1,0:T(8,128)S(1)}, f32[296,128]{1,0:T(8,128)S(1)}, u32[]{:S(2)}, u32[]{:S(2)}) collective-permute-start(f32[296,128]{1,0:T(8,128)S(1)} %get-tuple-element.17), channel_id=1, source_target_pairs={{0,16},{1,9},{2,18},{3,11},{4,20},{5,13},{6,22},{7,15},{8,24},{9,1... | collective-permute-start | bytes 454664 | tf_op jit(solution)/shard_map/ppermute | solution.py:35
  24.3 2.8 %copy-start.1 = (bf16[16,1152]{1,0:T(8,128)(2,1)S(1)}, bf16[16,1152]{1,0:T(8,128)(2,1)}, u32[]{:S(2)}) copy-start(bf16[16,1152]{1,0:T(8,128)(2,1)} %images.3) | copy-start | bytes 110596
  24.3 2.8 %copy-start.3 = (bf16[16,1152]{1,0:T(8,128)(2,1)S(1)}, bf16[16,1152]{1,0:T(8,128)(2,1)}, u32[]{:S(2)}) copy-start(bf16[16,1152]{1,0:T(8,128)(2,1)} %texts.3) | copy-start | bytes 110596
  24.3 2.8 %collective-permute-start.8 = (f32[152,128]{1,0:T(8,128)S(1)}, f32[152,128]{1,0:T(8,128)S(1)}, u32[]{:S(2)}, u32[]{:S(2)}) collective-permute-start(f32[152,128]{1,0:T(8,128)S(1)} %get-tuple-element.23), channel_id=1, source_target_pairs={{0,1},{1,0},{2,3},{3,2},{4,5},{5,4},{6,7},{7,6},{8,9},{9,8},{10,11... | collective-permute-start | bytes 233480 | tf_op jit(solution)/shard_map/ppermute | solution.py:35

commit v2 on v1

--- a/solution.py
+++ b/solution.py
@@ -9,6 +9,8 @@
 
 AXES = ("blk", "grp")
 LANES = 128
+SCALE_TOP = 16.0
+FLOAT16_TOP = 65504.0
 VMEM_BYTES = 24 * 1024 * 1024
 
 
@@ -24,10 +26,9 @@
     need = half - len(top)
     image_bits = low[:need] + top
     text_bits = low[need:]
-    order = sorted(
-        range(1, 1 << half), key=lambda k: -bin(k).count("1")
-    )
-    return [(spread(k, image_bits), spread(k, text_bits)) for k in order]
+    return [
+        (spread(k, image_bits), spread(k ^ k >> 1, text_bits)) for k in range(1, 1 << half)
+    ]
 
 
 def permuted(value, devices, image_step, text_step):
@@ -39,29 +40,39 @@
     return lax.axis_index("grp") % 2 == 0
 
 
+def message_lift(count):
+    lift = 1.0
+    while lift * 2 * count * SCALE_TOP < FLOAT16_TOP:
+        lift *= 2
+    return lift
+
+
 def units(values):
     floats = values.astype(jnp.float32)
     norms = jnp.sqrt(jnp.sum(floats * floats, 1, keepdims=True) + 1e-06)
     return floats / norms, norms
 
 
-def embed_kernel(images, texts, keep, send):
-    image_emb = units(images[...])[0].astype(jnp.bfloat16)
-    text_emb = units(texts[...])[0].astype(jnp.bfloat16)
+def embed_kernel(own, images_near, texts_near, chip):
+    rows = own.shape[0]
+
+    def embed(raw):
+        return units(raw[...])[0].astype(jnp.bfloat16)
+
     first = first_core()
 
     @pl.when(first)
     def _():
-        keep[...] = image_emb
-        send[...] = text_emb
+        chip[:rows, :] = embed(own)
+        chip[rows:, :] = embed(images_near)
 
     @pl.when(jnp.logical_not(first))
     def _():
-        keep[...] = text_emb
-        send[...] = image_emb
+        chip[:rows, :] = embed(texts_near)
+        chip[rows:, :] = embed(own)
 
 
-def tile_kernel(rows, total, scale_ref, shift_ref, mine, other, *outs):
+def tile_kernel(rows, scale_ref, shift_ref, mine, other, *outs):
     scale = scale_ref[0]
     shift = shift_ref[0]
     own = mine[...]
@@ -79,7 +90,7 @@
     turned = scale * lax.dot_general(far, own, nt, preferred_element_type=jnp.float32) + shift
     signed = turned * (1.0 - 2.0 * label)
     soft = jnp.maximum(signed, 0.0) + jnp.log1p(jnp.exp(-jnp.abs(signed)))
-    loss = jnp.sum(soft, 0, keepdims=True) / total
+    loss = jnp.sum(soft, 0, keepdims=True)
     chunks = own.shape[1] // LANES
     for slot, out in enumerate(outs):
         for core in range(2):
@@ -95,7 +106,7 @@
         out[2 * chunks * rows :, :] = part
 
 
-def finish_kernel(images, texts, kept, came, loss_out, image_out, text_out):
+def finish_kernel(total, images, texts, kept, came, loss_out, image_out, text_out):
     rows, width = images.shape
     chunks = width // LANES
     first = first_core()
@@ -109,13 +120,13 @@
 
     @pl.when(first)
     def _():
-        loss_out[...] = kept[chunks * rows : chunks * rows + 1, :]
+        loss_out[...] = kept[chunks * rows, :rows] / total
         image_out[...] = back(images, kept)
         text_out[...] = back(texts, came)
 
     @pl.when(jnp.logical_not(first))
     def _():
-        loss_out[...] = pltpu.roll(came[chunks * rows :, :], LANES - rows, 1)[:1]
+        loss_out[...] = pltpu.roll(came[chunks * rows :, :], LANES - rows, 1)[0, :rows] / total
         image_out[...] = back(images, came)
         text_out[...] = back(texts, kept)
 
@@ -131,42 +142,42 @@
     steps = plan(blocks, groups)
     chunks = width // LANES
     first = first_core()
-    piece = jax.ShapeDtypeStruct((rows, width), jnp.bfloat16)
-    keep, send = pl.pallas_call(
+    images_near = permuted(images, devices, 1, 1)
+    texts_near = permuted(texts, devices, 1, 1)
+    chip = pl.pallas_call(
         embed_kernel,
-        out_shape=(piece, piece),
-        in_specs=vmem(2),
-        out_specs=tuple(vmem(2)),
+        out_shape=jax.ShapeDtypeStruct((2 * rows, width), jnp.bfloat16),
+        in_specs=vmem(3),
+        out_specs=vmem(1)[0],
         compiler_params=params,
         name="embed",
-    )(images, texts)
-    got = permuted(send, devices, 1, 1)
-    chip = jnp.where(first, jnp.concatenate([keep, got], 0), jnp.concatenate([got, keep], 0))
-    gathered = [permuted(chip, devices, a, b) for a, b in reversed(steps)][::-1]
+    )(jnp.where(first, images, texts), images_near, texts_near)
+    gathered = [permuted(chip, devices, a, b) for a, b in steps]
     mine = jnp.concatenate([chip] + gathered, 0)
     other = permuted(mine, devices, 1, 1)
     message = jax.ShapeDtypeStruct((2 * chunks * rows + 8, LANES), jnp.float32)
     parts = pl.pallas_call(
-        functools.partial(tile_kernel, rows, devices * rows),
+        functools.partial(tile_kernel, rows),
         out_shape=[message] * (len(steps) + 1),
         in_specs=[pl.BlockSpec(memory_space=pltpu.SMEM)] * 2 + vmem(2),
         out_specs=vmem(len(steps) + 1),
         compiler_params=params,
         name="tile",
     )(scale.reshape(1), shift.reshape(1), mine, other)
-    arrived = [permuted(part, devices, a, b) for part, (a, b) in zip(parts[1:], steps)]
+    lift = message_lift(2 * rows << len(steps).bit_length())
     whole = parts[0]
-    for part in arrived:
-        whole = whole + part
+    for part, (a, b) in zip(parts[1:], steps):
+        sent = (part * lift).astype(jnp.float16)
+        whole = whole + permuted(sent, devices, a, b).astype(jnp.float32) * (1.0 / lift)
     half = chunks * rows
     upper, lower, tail = whole[:half], whole[half : 2 * half], whole[2 * half :]
     kept = jnp.concatenate([jnp.where(first, upper, lower), tail], 0)
     leaving = jnp.concatenate([jnp.where(first, lower, upper), tail], 0)
     came = permuted(leaving, devices, 1, 1)
     loss, image_grad, text_grad = pl.pallas_call(
-        finish_kernel,
+        functools.partial(finish_kernel, devices * rows),
         out_shape=(
-            jax.ShapeDtypeStruct((1, LANES), jnp.float32),
+            jax.ShapeDtypeStruct((rows,), jnp.float32),
             jax.ShapeDtypeStruct((rows, width), jnp.float32),
             jax.ShapeDtypeStruct((rows, width), jnp.float32),
         ),
@@ -175,7 +186,7 @@
         compiler_params=params,
         name="finish",
     )(images, texts, kept, came)
-    return loss[0, :rows], image_grad, text_grad
+    return loss, image_grad, text_grad
 
 
 def solution(mesh):

time: 28.7 us -> 23.9 us (0.83)
  local copies, waits for them, and re-layouts: 2.06 us -> 0.02 us
  waiting for transfers between devices: 11.7 us -> 9.76 us
  starting transfers between devices: 10.9 us -> 9.19 us
  other arithmetic: 0.12 us -> 0.94 us
    ppermute x9 -> x10, waiting for transfers between devices: 11.7 us -> 9.76 us  [permuted(): return lax.ppermute(value, AXES, pairs)]
    ppermute x9 -> x10, starting transfers between devices: 10.9 us -> 9.19 us  [permuted(): return lax.ppermute(value, AXES, pairs)]
    unnamed x8 -> x4, local copies, waits for them, and re-layouts: 1.54 us -> 0.01 us
    select_n x1, other arithmetic: 0.02 us -> 0.78 us  [local(): jnp.where(first, images, texts)]
    squeeze x1 -> x0, local copies, waits for them, and re-layouts: 0.51 us -> none  [local(): return (loss[0, :rows], image_grad, text_grad)]
  transfers between devices with their start and end apart: 9 -> 10, of which waited for: 8 -> 9; matrix products, arithmetic and copies ran while one was open for 0% -> 3% of each run, Pallas kernels for 0% -> 0%
where the time goes in v2:
time: 23.9 us; the launch traced here: 23.7 us
  waiting for transfers between devices  9.76 us (41%)
  starting transfers between devices  9.19 us (38%)
  between operations  2.03 us (8%)
  Pallas kernels  1.76 us (7%)
  other arithmetic  0.94 us (4%)
    ppermute x10, waiting for transfers between devices, permuted(): return lax.ppermute(value, AXES, pairs)  9.76 us
    ppermute x10, starting transfers between devices, permuted(): return lax.ppermute(value, AXES, pairs)  9.19 us
    pallas_call x1, Pallas kernels, local(): pl.pallas_call(functools.partial(finish_kernel, devices * rows), out_shap...  0.87 us
    select_n x1, other arithmetic, local(): jnp.where(first, images, texts)  0.78 us
    pallas_call x1, Pallas kernels, local(): pl.pallas_call(functools.partial(tile_kernel, rows), out_shape=[message]...  0.77 us
  transfers between devices with their start and end apart: 10, of which 9 were waited for; matrix products, arithmetic and copies ran while one was open for 3% of the time, Pallas kernels for 0%

profile of v2, /device:TPU:0, one launch (start us, length us, event | category | flops | bytes accessed | tf_op | source)
XLA Modules:
  0.0 23.7 jit_solution(1799855668339737559)
XLA Ops:
  0.6 0.5 %collective-permute-start = (bf16[16,1152]{1,0:T(8,128)(2,1)}, bf16[16,1152]{1,0:T(8,128)(2,1)S(1)}, u32[]{:S(2)}, u32[]{:S(2)}) collective-permute-start(bf16[16,1152]{1,0:T(8,128)(2,1)} %images.1), channel_id=1, source_target_pairs={{0,1},{1,0},{2,3},{3,2},{4,5},{5,4},{6,7},{7,6},{8,9},{9,8},{10,11... | collective-permute-start | bytes 110600 | tf_op jit(solution)/shard_map/ppermute | solution.py:36
  1.1 0.1 collective-permute-start.1
  1.2 0.8 %broadcast_select_fusion.own = bf16[16,1152]{1,0:T(8,128)(2,1)S(1)} fusion(bf16[16,1152]{1,0:T(8,128)(2,1)} %images.1, bf16[16,1152]{1,0:T(8,128)(2,1)} %texts.1, pred[]{:T(512)S(6)} %eq.5), kind=kLoop, calls=%fused_computation.9 | loop fusion | flops 18432 | bytes 110593 | tf_op jit(solution)/shard_map/jit(_where)/select_n | solution.py:154
  2.0 0.2 collective-permute-done.images_near
  2.2 0.3 %collective-permute-done.1.texts_near = bf16[16,1152]{1,0:T(8,128)(2,1)S(1)} collective-permute-done((bf16[16,1152]{1,0:T(8,128)(2,1)}, bf16[16,1152]{1,0:T(8,128)(2,1)S(1)}, u32[]{:S(2)}, u32[]{:S(2)}) %collective-permute-start.1) | collective-permute-done | bytes 36896 | tf_op jit(solution)/shard_map/ppermute | solution.py:36
  2.6 0.1 embed.1
  2.7 3.7 %collective-permute-start.4 = (bf16[32,1152]{1,0:T(8,128)(2,1)S(1)}, bf16[32,1152]{1,0:T(8,128)(2,1)S(1)}, u32[]{:S(2)}, u32[]{:S(2)}) collective-permute-start(bf16[32,1152]{1,0:T(8,128)(2,1)S(1)} %embed.1), channel_id=1, source_target_pairs={{0,18},{1,9},{2,16},{3,11},{4,22},{5,13},{6,20},{7,15},{8,26},{9,1... | collective-permute-start | bytes 221192 | tf_op jit(solution)/shard_map/ppermute | solution.py:36
  6.4 0.5 %collective-permute-start.3 = (bf16[32,1152]{1,0:T(8,128)(2,1)S(1)}, bf16[32,1152]{1,0:T(8,128)(2,1)S(1)}, u32[]{:S(2)}, u32[]{:S(2)}) collective-permute-start(bf16[32,1152]{1,0:T(8,128)(2,1)S(1)} %embed.1), channel_id=1, source_target_pairs={{0,16},{1,13},{2,18},{3,15},{4,20},{5,9},{6,22},{7,11},{8,24},{9,5... | collective-permute-start | bytes 221192 | tf_op jit(solution)/shard_map/ppermute | solution.py:36
  6.9 0.1 collective-permute-start.2
  7.0 1.7 %collective-permute-done.4 = bf16[32,1152]{1,0:T(8,128)(2,1)S(1)} collective-permute-done((bf16[32,1152]{1,0:T(8,128)(2,1)S(1)}, bf16[32,1152]{1,0:T(8,128)(2,1)S(1)}, u32[]{:S(2)}, u32[]{:S(2)}) %collective-permute-start.4) | collective-permute-done | bytes 73760 | tf_op jit(solution)/shard_map/ppermute | solution.py:36
  8.7 2.0 %collective-permute-done.3 = bf16[32,1152]{1,0:T(8,128)(2,1)S(1)} collective-permute-done((bf16[32,1152]{1,0:T(8,128)(2,1)S(1)}, bf16[32,1152]{1,0:T(8,128)(2,1)S(1)}, u32[]{:S(2)}, u32[]{:S(2)}) %collective-permute-start.3) | collective-permute-done | bytes 73760 | tf_op jit(solution)/shard_map/ppermute | solution.py:36
  10.7 0.5 %collective-permute-done.2 = bf16[32,1152]{1,0:T(8,128)(2,1)S(1)} collective-permute-done((bf16[32,1152]{1,0:T(8,128)(2,1)S(1)}, bf16[32,1152]{1,0:T(8,128)(2,1)S(1)}, u32[]{:S(2)}, u32[]{:S(2)}) %collective-permute-start.2) | collective-permute-done | bytes 73760 | tf_op jit(solution)/shard_map/ppermute | solution.py:36
  11.3 0.5 %collective-permute-start.5 = (bf16[128,1152]{1,0:T(8,128)(2,1)S(1)}, bf16[128,1152]{1,0:T(8,128)(2,1)S(1)}, u32[]{:S(2)}, u32[]{:S(2)}) collective-permute-start(bf16[128,1152]{1,0:T(8,128)(2,1)S(1)} %pad_maximum_fusion.mine), channel_id=1, source_target_pairs={{0,1},{1,0},{2,3},{3,2},{4,5},{5,4},{6,7},{7,6},{8,9},{9,8},{10,11... | collective-permute-start | bytes 884744 | tf_op jit(solution)/shard_map/ppermute | solution.py:36
  13.1 0.0 collective-permute-done.5.other
  13.1 0.8 %tile.1 = (f32[296,128]{1,0:T(8,128)S(1)}, f32[296,128]{1,0:T(8,128)S(1)}, f32[296,128]{1,0:T(8,128)S(1)}, f32[296,128]{1,0:T(8,128)S(1)}) custom-call(f32[1]{0:T(128)} %bitcast.2.scale_ref, f32[1]{0:T(128)} %bitcast.3.shift_ref, bf16[128,1152]{1,0:T(8,128)(2,1)S(1)} %pad_maximum_fusion.mine, bf16[128,1152]{1,0:T(8,128)(2,1)S(1)} %collective-permute-done.5.other), custom_call_target="tpu_custom_call" | custom-call | tf_op jit(solution)/shard_map/tile/pallas_call | solution.py:159
  13.9 2.5 %collective-permute-start.8 = (f16[296,128]{1,0:T(8,128)(2,1)S(1)}, f16[296,128]{1,0:T(8,128)(2,1)S(1)}, u32[]{:S(2)}, u32[]{:S(2)}) collective-permute-start(f16[296,128]{1,0:T(8,128)(2,1)S(1)} %multiply_convert_fusion), channel_id=1, source_target_pairs={{0,18},{1,9},{2,16},{3,11},{4,22},{5,13},{6,20},{7,15},{8,26},{9,1... | collective-permute-start | bytes 227336 | tf_op jit(solution)/shard_map/ppermute | solution.py:36
  16.4 0.5 %collective-permute-start.7 = (f16[296,128]{1,0:T(8,128)(2,1)S(1)}, f16[296,128]{1,0:T(8,128)(2,1)S(1)}, u32[]{:S(2)}, u32[]{:S(2)}) collective-permute-start(f16[296,128]{1,0:T(8,128)(2,1)S(1)} %multiply_convert_fusion.1), channel_id=1, source_target_pairs={{0,16},{1,13},{2,18},{3,15},{4,20},{5,9},{6,22},{7,11},{8,24},{9,5... | collective-permute-start | bytes 227336 | tf_op jit(solution)/shard_map/ppermute | solution.py:36
  17.0 0.5 %collective-permute-start.6 = (f16[296,128]{1,0:T(8,128)(2,1)S(1)}, f16[296,128]{1,0:T(8,128)(2,1)S(1)}, u32[]{:S(2)}, u32[]{:S(2)}) collective-permute-start(f16[296,128]{1,0:T(8,128)(2,1)S(1)} %multiply_convert_fusion.2), channel_id=1, source_target_pairs={{0,2},{1,5},{2,0},{3,7},{4,6},{5,1},{6,4},{7,3},{8,10},{9,13},{10,... | collective-permute-start | bytes 227336 | tf_op jit(solution)/shard_map/ppermute | solution.py:36
  17.5 1.8 %collective-permute-done.8 = f16[296,128]{1,0:T(8,128)(2,1)S(1)} collective-permute-done((f16[296,128]{1,0:T(8,128)(2,1)S(1)}, f16[296,128]{1,0:T(8,128)(2,1)S(1)}, u32[]{:S(2)}, u32[]{:S(2)}) %collective-permute-start.8) | collective-permute-done | bytes 75808 | tf_op jit(solution)/shard_map/ppermute | solution.py:36
  19.3 1.5 %collective-permute-done.7 = f16[296,128]{1,0:T(8,128)(2,1)S(1)} collective-permute-done((f16[296,128]{1,0:T(8,128)(2,1)S(1)}, f16[296,128]{1,0:T(8,128)(2,1)S(1)}, u32[]{:S(2)}, u32[]{:S(2)}) %collective-permute-start.7) | collective-permute-done | bytes 75808 | tf_op jit(solution)/shard_map/ppermute | solution.py:36
  20.8 0.5 %collective-permute-done.6 = f16[296,128]{1,0:T(8,128)(2,1)S(1)} collective-permute-done((f16[296,128]{1,0:T(8,128)(2,1)S(1)}, f16[296,128]{1,0:T(8,128)(2,1)S(1)}, u32[]{:S(2)}, u32[]{:S(2)}) %collective-permute-start.6) | collective-permute-done | bytes 75808 | tf_op jit(solution)/shard_map/ppermute | solution.py:36
  21.3 0.1 multiply_add_fusion
  21.4 0.0 copy-start
  21.4 0.0 copy-start.1
  21.5 0.3 %collective-permute-start.9 = (f32[152,128]{1,0:T(8,128)S(1)}, f32[152,128]{1,0:T(8,128)S(1)}, u32[]{:S(2)}, u32[]{:S(2)}) collective-permute-start(f32[152,128]{1,0:T(8,128)S(1)} %get-tuple-element.13), channel_id=1, source_target_pairs={{0,1},{1,0},{2,3},{3,2},{4,5},{5,4},{6,7},{7,6},{8,9},{9,8},{10,11... | collective-permute-start | bytes 233480 | tf_op jit(solution)/shard_map/ppermute | solution.py:36
  21.7 1.1 %collective-permute-done.9.came = f32[152,128]{1,0:T(8,128)S(1)} collective-permute-done((f32[152,128]{1,0:T(8,128)S(1)}, f32[152,128]{1,0:T(8,128)S(1)}, u32[]{:S(2)}, u32[]{:S(2)}) %collective-permute-start.9) | collective-permute-done | bytes 77856 | tf_op jit(solution)/shard_map/ppermute | solution.py:36
  22.8 0.0 copy-done
  22.8 0.0 copy-done.1
  22.8 0.9 %finish.1 = (f32[16]{0:T(128)}, f32[16,1152]{1,0:T(8,128)}, f32[16,1152]{1,0:T(8,128)}) custom-call(bf16[16,1152]{1,0:T(8,128)(2,1)S(1)} %copy-done, bf16[16,1152]{1,0:T(8,128)(2,1)S(1)} %copy-done.1, f32[152,128]{1,0:T(8,128)S(1)} %get-tuple-element.14.kept, f32[152,128]{1,0:T(8,128)S(1)} %collective-permute-done.9.came), custom_call_target="tpu_custom_call" | custom-call | tf_op jit(solution)/shard_map/finish/pallas_call | solution.py:177
  (7 shorter events, 0.1 us)
Async XLA Ops:
  0.6 1.6 %collective-permute-start = (bf16[16,1152]{1,0:T(8,128)(2,1)}, bf16[16,1152]{1,0:T(8,128)(2,1)S(1)}, u32[]{:S(2)}, u32[]{:S(2)}) collective-permute-start(bf16[16,1152]{1,0:T(8,128)(2,1)} %images.1), channel_id=1, source_target_pairs={{0,1},{1,0},{2,3},{3,2},{4,5},{5,4},{6,7},{7,6},{8,9},{9,8},{10,11... | collective-permute-start | bytes 110600 | tf_op jit(solution)/shard_map/ppermute | solution.py:36
  1.1 1.4 %collective-permute-start.1 = (bf16[16,1152]{1,0:T(8,128)(2,1)}, bf16[16,1152]{1,0:T(8,128)(2,1)S(1)}, u32[]{:S(2)}, u32[]{:S(2)}) collective-permute-start(bf16[16,1152]{1,0:T(8,128)(2,1)} %texts.1), channel_id=1, source_target_pairs={{0,1},{1,0},{2,3},{3,2},{4,5},{5,4},{6,7},{7,6},{8,9},{9,8},{10,11... | collective-permute-start | bytes 110600 | tf_op jit(solution)/shard_map/ppermute | solution.py:36
  2.7 6.0 %collective-permute-start.4 = (bf16[32,1152]{1,0:T(8,128)(2,1)S(1)}, bf16[32,1152]{1,0:T(8,128)(2,1)S(1)}, u32[]{:S(2)}, u32[]{:S(2)}) collective-permute-start(bf16[32,1152]{1,0:T(8,128)(2,1)S(1)} %embed.1), channel_id=1, source_target_pairs={{0,18},{1,9},{2,16},{3,11},{4,22},{5,13},{6,20},{7,15},{8,26},{9,1... | collective-permute-start | bytes 221192 | tf_op jit(solution)/shard_map/ppermute | solution.py:36
  6.4 4.4 %collective-permute-start.3 = (bf16[32,1152]{1,0:T(8,128)(2,1)S(1)}, bf16[32,1152]{1,0:T(8,128)(2,1)S(1)}, u32[]{:S(2)}, u32[]{:S(2)}) collective-permute-start(bf16[32,1152]{1,0:T(8,128)(2,1)S(1)} %embed.1), channel_id=1, source_target_pairs={{0,16},{1,13},{2,18},{3,15},{4,20},{5,9},{6,22},{7,11},{8,24},{9,5... | collective-permute-start | bytes 221192 | tf_op jit(solution)/shard_map/ppermute | solution.py:36
  6.9 4.4 %collective-permute-start.2 = (bf16[32,1152]{1,0:T(8,128)(2,1)S(1)}, bf16[32,1152]{1,0:T(8,128)(2,1)S(1)}, u32[]{:S(2)}, u32[]{:S(2)}) collective-permute-start(bf16[32,1152]{1,0:T(8,128)(2,1)S(1)} %embed.1), channel_id=1, source_target_pairs={{0,2},{1,5},{2,0},{3,7},{4,6},{5,1},{6,4},{7,3},{8,10},{9,13},{10,... | collective-permute-start | bytes 221192 | tf_op jit(solution)/shard_map/ppermute | solution.py:36
  11.3 1.8 %collective-permute-start.5 = (bf16[128,1152]{1,0:T(8,128)(2,1)S(1)}, bf16[128,1152]{1,0:T(8,128)(2,1)S(1)}, u32[]{:S(2)}, u32[]{:S(2)}) collective-permute-start(bf16[128,1152]{1,0:T(8,128)(2,1)S(1)} %pad_maximum_fusion.mine), channel_id=1, source_target_pairs={{0,1},{1,0},{2,3},{3,2},{4,5},{5,4},{6,7},{7,6},{8,9},{9,8},{10,11... | collective-permute-start | bytes 884744 | tf_op jit(solution)/shard_map/ppermute | solution.py:36
  13.9 5.3 %collective-permute-start.8 = (f16[296,128]{1,0:T(8,128)(2,1)S(1)}, f16[296,128]{1,0:T(8,128)(2,1)S(1)}, u32[]{:S(2)}, u32[]{:S(2)}) collective-permute-start(f16[296,128]{1,0:T(8,128)(2,1)S(1)} %multiply_convert_fusion), channel_id=1, source_target_pairs={{0,18},{1,9},{2,16},{3,11},{4,22},{5,13},{6,20},{7,15},{8,26},{9,1... | collective-permute-start | bytes 227336 | tf_op jit(solution)/shard_map/ppermute | solution.py:36
  16.4 4.4 %collective-permute-start.7 = (f16[296,128]{1,0:T(8,128)(2,1)S(1)}, f16[296,128]{1,0:T(8,128)(2,1)S(1)}, u32[]{:S(2)}, u32[]{:S(2)}) collective-permute-start(f16[296,128]{1,0:T(8,128)(2,1)S(1)} %multiply_convert_fusion.1), channel_id=1, source_target_pairs={{0,16},{1,13},{2,18},{3,15},{4,20},{5,9},{6,22},{7,11},{8,24},{9,5... | collective-permute-start | bytes 227336 | tf_op jit(solution)/shard_map/ppermute | solution.py:36
  17.0 4.4 %collective-permute-start.6 = (f16[296,128]{1,0:T(8,128)(2,1)S(1)}, f16[296,128]{1,0:T(8,128)(2,1)S(1)}, u32[]{:S(2)}, u32[]{:S(2)}) collective-permute-start(f16[296,128]{1,0:T(8,128)(2,1)S(1)} %multiply_convert_fusion.2), channel_id=1, source_target_pairs={{0,2},{1,5},{2,0},{3,7},{4,6},{5,1},{6,4},{7,3},{8,10},{9,13},{10,... | collective-permute-start | bytes 227336 | tf_op jit(solution)/shard_map/ppermute | solution.py:36
  21.4 1.4 %copy-start = (bf16[16,1152]{1,0:T(8,128)(2,1)S(1)}, bf16[16,1152]{1,0:T(8,128)(2,1)}, u32[]{:S(2)}) copy-start(bf16[16,1152]{1,0:T(8,128)(2,1)} %images.1) | copy-start | bytes 110596
  21.4 1.4 %copy-start.1 = (bf16[16,1152]{1,0:T(8,128)(2,1)S(1)}, bf16[16,1152]{1,0:T(8,128)(2,1)}, u32[]{:S(2)}) copy-start(bf16[16,1152]{1,0:T(8,128)(2,1)} %texts.1) | copy-start | bytes 110596
  21.5 1.3 %collective-permute-start.9 = (f32[152,128]{1,0:T(8,128)S(1)}, f32[152,128]{1,0:T(8,128)S(1)}, u32[]{:S(2)}, u32[]{:S(2)}) collective-permute-start(f32[152,128]{1,0:T(8,128)S(1)} %get-tuple-element.13), channel_id=1, source_target_pairs={{0,1},{1,0},{2,3},{3,2},{4,5},{5,4},{6,7},{7,6},{8,9},{9,8},{10,11... | collective-permute-start | bytes 233480 | tf_op jit(solution)/shard_map/ppermute | solution.py:36

commit v3 on v2

--- a/solution.py
+++ b/solution.py
@@ -24,11 +24,9 @@
     top = [bit for bit in bits if bit >= groups]
     low = [bit for bit in bits if bit < groups]
     need = half - len(top)
-    image_bits = low[:need] + top
+    image_bits = top + low[:need]
     text_bits = low[need:]
-    return [
-        (spread(k, image_bits), spread(k ^ k >> 1, text_bits)) for k in range(1, 1 << half)
-    ]
+    return [(spread(k, image_bits), spread(k, text_bits)) for k in range(1, 1 << half)]
 
 
 def permuted(value, devices, image_step, text_step):
@@ -87,10 +85,9 @@
     logit = scale * lax.dot_general(own, far, nt, preferred_element_type=jnp.float32) + shift
     coef = ((jax.nn.sigmoid(logit) - label) * scale).astype(jnp.bfloat16)
     grad = jnp.dot(coef, far, preferred_element_type=jnp.float32)
-    turned = scale * lax.dot_general(far, own, nt, preferred_element_type=jnp.float32) + shift
-    signed = turned * (1.0 - 2.0 * label)
+    signed = logit * (1.0 - 2.0 * label)
     soft = jnp.maximum(signed, 0.0) + jnp.log1p(jnp.exp(-jnp.abs(signed)))
-    loss = jnp.sum(soft, 0, keepdims=True)
+    loss = jnp.sum(soft.T, 0, keepdims=True)
     chunks = own.shape[1] // LANES
     for slot, out in enumerate(outs):
         for core in range(2):

time: 23.9 us -> 23.7 us (level)
  no operation moved by 1% of the time
where the time goes in v3:
time: 23.7 us; the launch traced here: 23.5 us
  waiting for transfers between devices  9.72 us (41%)
  starting transfers between devices  9.22 us (39%)
  between operations  2.03 us (9%)
  Pallas kernels  1.53 us (6%)
  other arithmetic  0.94 us (4%)
    ppermute x10, waiting for transfers between devices, permuted(): return lax.ppermute(value, AXES, pairs)  9.72 us
    ppermute x10, starting transfers between devices, permuted(): return lax.ppermute(value, AXES, pairs)  9.22 us
    pallas_call x1, Pallas kernels, local(): pl.pallas_call(functools.partial(finish_kernel, devices * rows), out_shap...  0.87 us
    select_n x1, other arithmetic, local(): jnp.where(first, images, texts)  0.78 us
    pallas_call x1, Pallas kernels, local(): pl.pallas_call(functools.partial(tile_kernel, rows), out_shape=[message]...  0.54 us
  transfers between devices with their start and end apart: 10, of which 9 were waited for; matrix products, arithmetic and copies ran while one was open for 3% of the time, Pallas kernels for 0%

profile of v3, /device:TPU:0, one launch (start us, length us, event | category | flops | bytes accessed | tf_op | source)
XLA Modules:
  0.0 23.5 jit_solution(2558794372565616548)
XLA Ops:
  0.6 0.5 %collective-permute-start = (bf16[16,1152]{1,0:T(8,128)(2,1)}, bf16[16,1152]{1,0:T(8,128)(2,1)S(1)}, u32[]{:S(2)}, u32[]{:S(2)}) collective-permute-start(bf16[16,1152]{1,0:T(8,128)(2,1)} %images.1), channel_id=1, source_target_pairs={{0,1},{1,0},{2,3},{3,2},{4,5},{5,4},{6,7},{7,6},{8,9},{9,8},{10,11... | collective-permute-start | bytes 110600 | tf_op jit(solution)/shard_map/ppermute | solution.py:34
  1.1 0.1 collective-permute-start.1
  1.2 0.8 %broadcast_select_fusion.own = bf16[16,1152]{1,0:T(8,128)(2,1)S(1)} fusion(bf16[16,1152]{1,0:T(8,128)(2,1)} %images.1, bf16[16,1152]{1,0:T(8,128)(2,1)} %texts.1, pred[]{:T(512)S(6)} %eq.5), kind=kLoop, calls=%fused_computation.9 | loop fusion | flops 18432 | bytes 110593 | tf_op jit(solution)/shard_map/jit(_where)/select_n | solution.py:151
  2.0 0.2 collective-permute-done.images_near
  2.2 0.3 %collective-permute-done.1.texts_near = bf16[16,1152]{1,0:T(8,128)(2,1)S(1)} collective-permute-done((bf16[16,1152]{1,0:T(8,128)(2,1)}, bf16[16,1152]{1,0:T(8,128)(2,1)S(1)}, u32[]{:S(2)}, u32[]{:S(2)}) %collective-permute-start.1) | collective-permute-done | bytes 36896 | tf_op jit(solution)/shard_map/ppermute | solution.py:34
  2.6 0.1 embed.1
  2.7 3.7 %collective-permute-start.4 = (bf16[32,1152]{1,0:T(8,128)(2,1)S(1)}, bf16[32,1152]{1,0:T(8,128)(2,1)S(1)}, u32[]{:S(2)}, u32[]{:S(2)}) collective-permute-start(bf16[32,1152]{1,0:T(8,128)(2,1)S(1)} %embed.1), channel_id=1, source_target_pairs={{0,18},{1,13},{2,16},{3,15},{4,22},{5,9},{6,20},{7,11},{8,26},{9,5... | collective-permute-start | bytes 221192 | tf_op jit(solution)/shard_map/ppermute | solution.py:34
  6.4 0.5 %collective-permute-start.3 = (bf16[32,1152]{1,0:T(8,128)(2,1)S(1)}, bf16[32,1152]{1,0:T(8,128)(2,1)S(1)}, u32[]{:S(2)}, u32[]{:S(2)}) collective-permute-start(bf16[32,1152]{1,0:T(8,128)(2,1)S(1)} %embed.1), channel_id=1, source_target_pairs={{0,2},{1,9},{2,0},{3,11},{4,6},{5,13},{6,4},{7,15},{8,10},{9,1},{1... | collective-permute-start | bytes 221192 | tf_op jit(solution)/shard_map/ppermute | solution.py:34
  6.9 0.1 collective-permute-start.2
  7.0 1.7 %collective-permute-done.4 = bf16[32,1152]{1,0:T(8,128)(2,1)S(1)} collective-permute-done((bf16[32,1152]{1,0:T(8,128)(2,1)S(1)}, bf16[32,1152]{1,0:T(8,128)(2,1)S(1)}, u32[]{:S(2)}, u32[]{:S(2)}) %collective-permute-start.4) | collective-permute-done | bytes 73760 | tf_op jit(solution)/shard_map/ppermute | solution.py:34
  8.7 2.0 %collective-permute-done.3 = bf16[32,1152]{1,0:T(8,128)(2,1)S(1)} collective-permute-done((bf16[32,1152]{1,0:T(8,128)(2,1)S(1)}, bf16[32,1152]{1,0:T(8,128)(2,1)S(1)}, u32[]{:S(2)}, u32[]{:S(2)}) %collective-permute-start.3) | collective-permute-done | bytes 73760 | tf_op jit(solution)/shard_map/ppermute | solution.py:34
  10.7 0.5 %collective-permute-done.2 = bf16[32,1152]{1,0:T(8,128)(2,1)S(1)} collective-permute-done((bf16[32,1152]{1,0:T(8,128)(2,1)S(1)}, bf16[32,1152]{1,0:T(8,128)(2,1)S(1)}, u32[]{:S(2)}, u32[]{:S(2)}) %collective-permute-start.2) | collective-permute-done | bytes 73760 | tf_op jit(solution)/shard_map/ppermute | solution.py:34
  11.3 0.5 %collective-permute-start.5 = (bf16[128,1152]{1,0:T(8,128)(2,1)S(1)}, bf16[128,1152]{1,0:T(8,128)(2,1)S(1)}, u32[]{:S(2)}, u32[]{:S(2)}) collective-permute-start(bf16[128,1152]{1,0:T(8,128)(2,1)S(1)} %pad_maximum_fusion.mine), channel_id=1, source_target_pairs={{0,1},{1,0},{2,3},{3,2},{4,5},{5,4},{6,7},{7,6},{8,9},{9,8},{10,11... | collective-permute-start | bytes 884744 | tf_op jit(solution)/shard_map/ppermute | solution.py:34
  13.1 0.0 collective-permute-done.5.other
  13.1 0.5 %tile.1 = (f32[296,128]{1,0:T(8,128)S(1)}, f32[296,128]{1,0:T(8,128)S(1)}, f32[296,128]{1,0:T(8,128)S(1)}, f32[296,128]{1,0:T(8,128)S(1)}) custom-call(f32[1]{0:T(128)} %bitcast.2.scale_ref, f32[1]{0:T(128)} %bitcast.3.shift_ref, bf16[128,1152]{1,0:T(8,128)(2,1)S(1)} %pad_maximum_fusion.mine, bf16[128,1152]{1,0:T(8,128)(2,1)S(1)} %collective-permute-done.5.other), custom_call_target="tpu_custom_call" | custom-call | tf_op jit(solution)/shard_map/tile/pallas_call | solution.py:156
  13.7 2.5 %collective-permute-start.8 = (f16[296,128]{1,0:T(8,128)(2,1)S(1)}, f16[296,128]{1,0:T(8,128)(2,1)S(1)}, u32[]{:S(2)}, u32[]{:S(2)}) collective-permute-start(f16[296,128]{1,0:T(8,128)(2,1)S(1)} %multiply_convert_fusion), channel_id=1, source_target_pairs={{0,18},{1,13},{2,16},{3,15},{4,22},{5,9},{6,20},{7,11},{8,26},{9,5... | collective-permute-start | bytes 227336 | tf_op jit(solution)/shard_map/ppermute | solution.py:34
  16.2 0.5 %collective-permute-start.7 = (f16[296,128]{1,0:T(8,128)(2,1)S(1)}, f16[296,128]{1,0:T(8,128)(2,1)S(1)}, u32[]{:S(2)}, u32[]{:S(2)}) collective-permute-start(f16[296,128]{1,0:T(8,128)(2,1)S(1)} %multiply_convert_fusion.1), channel_id=1, source_target_pairs={{0,2},{1,9},{2,0},{3,11},{4,6},{5,13},{6,4},{7,15},{8,10},{9,1},{1... | collective-permute-start | bytes 227336 | tf_op jit(solution)/shard_map/ppermute | solution.py:34
  16.7 0.5 %collective-permute-start.6 = (f16[296,128]{1,0:T(8,128)(2,1)S(1)}, f16[296,128]{1,0:T(8,128)(2,1)S(1)}, u32[]{:S(2)}, u32[]{:S(2)}) collective-permute-start(f16[296,128]{1,0:T(8,128)(2,1)S(1)} %multiply_convert_fusion.2), channel_id=1, source_target_pairs={{0,16},{1,5},{2,18},{3,7},{4,20},{5,1},{6,22},{7,3},{8,24},{9,13},... | collective-permute-start | bytes 227336 | tf_op jit(solution)/shard_map/ppermute | solution.py:34
  17.3 1.8 %collective-permute-done.8 = f16[296,128]{1,0:T(8,128)(2,1)S(1)} collective-permute-done((f16[296,128]{1,0:T(8,128)(2,1)S(1)}, f16[296,128]{1,0:T(8,128)(2,1)S(1)}, u32[]{:S(2)}, u32[]{:S(2)}) %collective-permute-start.8) | collective-permute-done | bytes 75808 | tf_op jit(solution)/shard_map/ppermute | solution.py:34
  19.1 1.5 %collective-permute-done.7 = f16[296,128]{1,0:T(8,128)(2,1)S(1)} collective-permute-done((f16[296,128]{1,0:T(8,128)(2,1)S(1)}, f16[296,128]{1,0:T(8,128)(2,1)S(1)}, u32[]{:S(2)}, u32[]{:S(2)}) %collective-permute-start.7) | collective-permute-done | bytes 75808 | tf_op jit(solution)/shard_map/ppermute | solution.py:34
  20.6 0.5 %collective-permute-done.6 = f16[296,128]{1,0:T(8,128)(2,1)S(1)} collective-permute-done((f16[296,128]{1,0:T(8,128)(2,1)S(1)}, f16[296,128]{1,0:T(8,128)(2,1)S(1)}, u32[]{:S(2)}, u32[]{:S(2)}) %collective-permute-start.6) | collective-permute-done | bytes 75808 | tf_op jit(solution)/shard_map/ppermute | solution.py:34
  21.1 0.1 multiply_add_fusion
  21.2 0.0 copy-start
  21.2 0.0 copy-start.1
  21.2 0.2 collective-permute-start.9
  21.5 1.1 %collective-permute-done.9.came = f32[152,128]{1,0:T(8,128)S(1)} collective-permute-done((f32[152,128]{1,0:T(8,128)S(1)}, f32[152,128]{1,0:T(8,128)S(1)}, u32[]{:S(2)}, u32[]{:S(2)}) %collective-permute-start.9) | collective-permute-done | bytes 77856 | tf_op jit(solution)/shard_map/ppermute | solution.py:34
  22.6 0.0 copy-done
  22.6 0.0 copy-done.1
  22.6 0.9 %finish.1 = (f32[16]{0:T(128)}, f32[16,1152]{1,0:T(8,128)}, f32[16,1152]{1,0:T(8,128)}) custom-call(bf16[16,1152]{1,0:T(8,128)(2,1)S(1)} %copy-done, bf16[16,1152]{1,0:T(8,128)(2,1)S(1)} %copy-done.1, f32[152,128]{1,0:T(8,128)S(1)} %get-tuple-element.14.kept, f32[152,128]{1,0:T(8,128)S(1)} %collective-permute-done.9.came), custom_call_target="tpu_custom_call" | custom-call | tf_op jit(solution)/shard_map/finish/pallas_call | solution.py:174
  (7 shorter events, 0.1 us)
Async XLA Ops:
  0.6 1.6 %collective-permute-start = (bf16[16,1152]{1,0:T(8,128)(2,1)}, bf16[16,1152]{1,0:T(8,128)(2,1)S(1)}, u32[]{:S(2)}, u32[]{:S(2)}) collective-permute-start(bf16[16,1152]{1,0:T(8,128)(2,1)} %images.1), channel_id=1, source_target_pairs={{0,1},{1,0},{2,3},{3,2},{4,5},{5,4},{6,7},{7,6},{8,9},{9,8},{10,11... | collective-permute-start | bytes 110600 | tf_op jit(solution)/shard_map/ppermute | solution.py:34
  1.1 1.4 %collective-permute-start.1 = (bf16[16,1152]{1,0:T(8,128)(2,1)}, bf16[16,1152]{1,0:T(8,128)(2,1)S(1)}, u32[]{:S(2)}, u32[]{:S(2)}) collective-permute-start(bf16[16,1152]{1,0:T(8,128)(2,1)} %texts.1), channel_id=1, source_target_pairs={{0,1},{1,0},{2,3},{3,2},{4,5},{5,4},{6,7},{7,6},{8,9},{9,8},{10,11... | collective-permute-start | bytes 110600 | tf_op jit(solution)/shard_map/ppermute | solution.py:34
  2.7 6.0 %collective-permute-start.4 = (bf16[32,1152]{1,0:T(8,128)(2,1)S(1)}, bf16[32,1152]{1,0:T(8,128)(2,1)S(1)}, u32[]{:S(2)}, u32[]{:S(2)}) collective-permute-start(bf16[32,1152]{1,0:T(8,128)(2,1)S(1)} %embed.1), channel_id=1, source_target_pairs={{0,18},{1,13},{2,16},{3,15},{4,22},{5,9},{6,20},{7,11},{8,26},{9,5... | collective-permute-start | bytes 221192 | tf_op jit(solution)/shard_map/ppermute | solution.py:34
  6.4 4.4 %collective-permute-start.3 = (bf16[32,1152]{1,0:T(8,128)(2,1)S(1)}, bf16[32,1152]{1,0:T(8,128)(2,1)S(1)}, u32[]{:S(2)}, u32[]{:S(2)}) collective-permute-start(bf16[32,1152]{1,0:T(8,128)(2,1)S(1)} %embed.1), channel_id=1, source_target_pairs={{0,2},{1,9},{2,0},{3,11},{4,6},{5,13},{6,4},{7,15},{8,10},{9,1},{1... | collective-permute-start | bytes 221192 | tf_op jit(solution)/shard_map/ppermute | solution.py:34
  6.9 4.4 %collective-permute-start.2 = (bf16[32,1152]{1,0:T(8,128)(2,1)S(1)}, bf16[32,1152]{1,0:T(8,128)(2,1)S(1)}, u32[]{:S(2)}, u32[]{:S(2)}) collective-permute-start(bf16[32,1152]{1,0:T(8,128)(2,1)S(1)} %embed.1), channel_id=1, source_target_pairs={{0,16},{1,5},{2,18},{3,7},{4,20},{5,1},{6,22},{7,3},{8,24},{9,13},... | collective-permute-start | bytes 221192 | tf_op jit(solution)/shard_map/ppermute | solution.py:34
  11.3 1.8 %collective-permute-start.5 = (bf16[128,1152]{1,0:T(8,128)(2,1)S(1)}, bf16[128,1152]{1,0:T(8,128)(2,1)S(1)}, u32[]{:S(2)}, u32[]{:S(2)}) collective-permute-start(bf16[128,1152]{1,0:T(8,128)(2,1)S(1)} %pad_maximum_fusion.mine), channel_id=1, source_target_pairs={{0,1},{1,0},{2,3},{3,2},{4,5},{5,4},{6,7},{7,6},{8,9},{9,8},{10,11... | collective-permute-start | bytes 884744 | tf_op jit(solution)/shard_map/ppermute | solution.py:34
  13.7 5.3 %collective-permute-start.8 = (f16[296,128]{1,0:T(8,128)(2,1)S(1)}, f16[296,128]{1,0:T(8,128)(2,1)S(1)}, u32[]{:S(2)}, u32[]{:S(2)}) collective-permute-start(f16[296,128]{1,0:T(8,128)(2,1)S(1)} %multiply_convert_fusion), channel_id=1, source_target_pairs={{0,18},{1,13},{2,16},{3,15},{4,22},{5,9},{6,20},{7,11},{8,26},{9,5... | collective-permute-start | bytes 227336 | tf_op jit(solution)/shard_map/ppermute | solution.py:34
  16.2 4.4 %collective-permute-start.7 = (f16[296,128]{1,0:T(8,128)(2,1)S(1)}, f16[296,128]{1,0:T(8,128)(2,1)S(1)}, u32[]{:S(2)}, u32[]{:S(2)}) collective-permute-start(f16[296,128]{1,0:T(8,128)(2,1)S(1)} %multiply_convert_fusion.1), channel_id=1, source_target_pairs={{0,2},{1,9},{2,0},{3,11},{4,6},{5,13},{6,4},{7,15},{8,10},{9,1},{1... | collective-permute-start | bytes 227336 | tf_op jit(solution)/shard_map/ppermute | solution.py:34
  16.7 4.4 %collective-permute-start.6 = (f16[296,128]{1,0:T(8,128)(2,1)S(1)}, f16[296,128]{1,0:T(8,128)(2,1)S(1)}, u32[]{:S(2)}, u32[]{:S(2)}) collective-permute-start(f16[296,128]{1,0:T(8,128)(2,1)S(1)} %multiply_convert_fusion.2), channel_id=1, source_target_pairs={{0,16},{1,5},{2,18},{3,7},{4,20},{5,1},{6,22},{7,3},{8,24},{9,13},... | collective-permute-start | bytes 227336 | tf_op jit(solution)/shard_map/ppermute | solution.py:34
  21.2 1.4 %copy-start = (bf16[16,1152]{1,0:T(8,128)(2,1)S(1)}, bf16[16,1152]{1,0:T(8,128)(2,1)}, u32[]{:S(2)}) copy-start(bf16[16,1152]{1,0:T(8,128)(2,1)} %images.1) | copy-start | bytes 110596
  21.2 1.4 %copy-start.1 = (bf16[16,1152]{1,0:T(8,128)(2,1)S(1)}, bf16[16,1152]{1,0:T(8,128)(2,1)}, u32[]{:S(2)}) copy-start(bf16[16,1152]{1,0:T(8,128)(2,1)} %texts.1) | copy-start | bytes 110596
  21.2 1.3 %collective-permute-start.9 = (f32[152,128]{1,0:T(8,128)S(1)}, f32[152,128]{1,0:T(8,128)S(1)}, u32[]{:S(2)}, u32[]{:S(2)}) collective-permute-start(f32[152,128]{1,0:T(8,128)S(1)} %get-tuple-element.13), channel_id=1, source_target_pairs={{0,1},{1,0},{2,3},{3,2},{4,5},{5,4},{6,7},{7,6},{8,9},{9,8},{10,11... | collective-permute-start | bytes 233480 | tf_op jit(solution)/shard_map/ppermute | solution.py:34

commit v4 on v3

--- a/solution.py
+++ b/solution.py
@@ -24,9 +24,10 @@
     top = [bit for bit in bits if bit >= groups]
     low = [bit for bit in bits if bit < groups]
     need = half - len(top)
-    image_bits = top + low[:need]
+    image_bits = low[:need] + top
     text_bits = low[need:]
-    return [(spread(k, image_bits), spread(k, text_bits)) for k in range(1, 1 << half)]
+    last = (1 << half) - 1
+    return [(spread(k, image_bits), spread(k, text_bits)) for k in [last, *range(1, last)]]
 
 
 def permuted(value, devices, image_step, text_step):
@@ -51,23 +52,23 @@
     return floats / norms, norms
 
 
-def embed_kernel(own, images_near, texts_near, chip):
-    rows = own.shape[0]
+def embed_kernel(flip, own, images_near, texts_near, chip):
+    rows = images_near.shape[0]
 
-    def embed(raw):
-        return units(raw[...])[0].astype(jnp.bfloat16)
+    def place(upper, lower):
+        chip[:rows, :] = units(upper)[0].astype(jnp.bfloat16)
+        chip[rows:, :] = units(lower)[0].astype(jnp.bfloat16)
 
     first = first_core()
+    images, texts = own[:rows, :], own[rows:, :]
 
     @pl.when(first)
     def _():
-        chip[:rows, :] = embed(own)
-        chip[rows:, :] = embed(images_near)
+        place(*((texts, texts_near[...]) if flip else (images, images_near[...])))
 
     @pl.when(jnp.logical_not(first))
     def _():
-        chip[:rows, :] = embed(texts_near)
-        chip[rows:, :] = embed(own)
+        place(*((images_near[...], images) if flip else (texts_near[...], texts)))
 
 
 def tile_kernel(rows, scale_ref, shift_ref, mine, other, *outs):
@@ -141,17 +142,21 @@
     first = first_core()
     images_near = permuted(images, devices, 1, 1)
     texts_near = permuted(texts, devices, 1, 1)
-    chip = pl.pallas_call(
-        embed_kernel,
-        out_shape=jax.ShapeDtypeStruct((2 * rows, width), jnp.bfloat16),
-        in_specs=vmem(3),
-        out_specs=vmem(1)[0],
-        compiler_params=params,
-        name="embed",
-    )(jnp.where(first, images, texts), images_near, texts_near)
+    own = jnp.concatenate([images, texts], 0)
+    chip, chip_other = [
+        pl.pallas_call(
+            functools.partial(embed_kernel, flip),
+            out_shape=jax.ShapeDtypeStruct((2 * rows, width), jnp.bfloat16),
+            in_specs=vmem(3),
+            out_specs=vmem(1)[0],
+            compiler_params=params,
+            name=name,
+        )(own, images_near, texts_near)
+        for flip, name in ((False, "embed"), (True, "embed_other"))
+    ]
     gathered = [permuted(chip, devices, a, b) for a, b in steps]
     mine = jnp.concatenate([chip] + gathered, 0)
-    other = permuted(mine, devices, 1, 1)
+    other = jnp.concatenate([chip_other] + [permuted(part, devices, 1, 1) for part in gathered], 0)
     message = jax.ShapeDtypeStruct((2 * chunks * rows + 8, LANES), jnp.float32)
     parts = pl.pallas_call(
         functools.partial(tile_kernel, rows),
@@ -163,7 +168,8 @@
     )(scale.reshape(1), shift.reshape(1), mine, other)
     lift = message_lift(2 * rows << len(steps).bit_length())
     whole = parts[0]
-    for part, (a, b) in zip(parts[1:], steps):
+    sends = list(zip(parts[1:], steps))
+    for part, (a, b) in sends[1:] + sends[:1]:
         sent = (part * lift).astype(jnp.float16)
         whole = whole + permuted(sent, devices, a, b).astype(jnp.float32) * (1.0 / lift)
     half = chunks * rows

time: 23.7 us -> 23.3 us (0.983)
  waiting for transfers between devices: 9.72 us -> 8.02 us
  starting transfers between devices: 9.22 us -> 10.4 us
  local copies, waits for them, and re-layouts: 0.02 us -> 0.79 us
  other arithmetic: 0.94 us -> 0.19 us
    ppermute x10 -> x12, waiting for transfers between devices: 9.72 us -> 8.02 us  [permuted(): return lax.ppermute(value, AXES, pairs)]
    ppermute x10 -> x12, starting transfers between devices: 9.22 us -> 10.4 us  [permuted(): return lax.ppermute(value, AXES, pairs)]
    select_n x1 -> x0, other arithmetic: 0.78 us -> none  [local(): jnp.where(first, images, texts)]
    unnamed x4 -> x5, local copies, waits for them, and re-layouts: 0.01 us -> 0.78 us
  transfers between devices with their start and end apart: 10 -> 12, of which waited for: 9 -> 11; matrix products, arithmetic and copies ran while one was open for 3% -> 4% of each run, Pallas kernels for 0% -> 1%
where the time goes in v4:
time: 23.3 us; the launch traced here: 23.1 us
  starting transfers between devices  10.4 us (45%)
  waiting for transfers between devices  8.02 us (34%)
  between operations  2.03 us (9%)
  Pallas kernels  1.66 us (7%)
  local copies, waits for them, and re-layouts  0.79 us (3%)
    ppermute x12, starting transfers between devices, permuted(): return lax.ppermute(value, AXES, pairs)  10.4 us
    ppermute x12, waiting for transfers between devices, permuted(): return lax.ppermute(value, AXES, pairs)  8.02 us
    pallas_call x1, Pallas kernels, local(): pl.pallas_call(functools.partial(finish_kernel, devices * rows), out_shap...  0.87 us
    unnamed x5, local copies, waits for them, and re-layouts  0.78 us
    pallas_call x1, Pallas kernels, local(): pl.pallas_call(functools.partial(tile_kernel, rows), out_shape=[message]...  0.54 us
  transfers between devices with their start and end apart: 12, of which 11 were waited for; matrix products, arithmetic and copies ran while one was open for 4% of the time, Pallas kernels for 1%

profile of v4, /device:TPU:0, one launch (start us, length us, event | category | flops | bytes accessed | tf_op | source)
XLA Modules:
  0.0 23.1 jit_solution(17179725127736297856)
XLA Ops:
  0.6 0.0 copy-start.1
  0.6 0.5 %collective-permute-start = (bf16[16,1152]{1,0:T(8,128)(2,1)}, bf16[16,1152]{1,0:T(8,128)(2,1)S(1)}, u32[]{:S(2)}, u32[]{:S(2)}) collective-permute-start(bf16[16,1152]{1,0:T(8,128)(2,1)} %images.1), channel_id=1, source_target_pairs={{0,1},{1,0},{2,3},{3,2},{4,5},{5,4},{6,7},{7,6},{8,9},{9,8},{10,11... | collective-permute-start | bytes 110600 | tf_op jit(solution)/shard_map/ppermute | solution.py:35
  1.2 0.1 collective-permute-start.1
  1.2 0.8 %constant_dynamic-update-slice_fusion.1 = bf16[32,1152]{1,0:T(8,128)(2,1)S(1)} fusion(bf16[16,1152]{1,0:T(8,128)(2,1)} %images.1), kind=kLoop, calls=%fused_computation.11 | loop fusion | bytes 73728
  2.0 0.0 copy-done.1
  2.0 0.2 collective-permute-done.images_near
  2.2 0.3 %collective-permute-done.1.texts_near = bf16[16,1152]{1,0:T(8,128)(2,1)S(1)} collective-permute-done((bf16[16,1152]{1,0:T(8,128)(2,1)}, bf16[16,1152]{1,0:T(8,128)(2,1)S(1)}, u32[]{:S(2)}, u32[]{:S(2)}) %collective-permute-start.1) | collective-permute-done | bytes 36896 | tf_op jit(solution)/shard_map/ppermute | solution.py:35
  2.6 0.1 embed.1
  2.7 3.7 %collective-permute-start.2 = (bf16[32,1152]{1,0:T(8,128)(2,1)S(1)}, bf16[32,1152]{1,0:T(8,128)(2,1)S(1)}, u32[]{:S(2)}, u32[]{:S(2)}) collective-permute-start(bf16[32,1152]{1,0:T(8,128)(2,1)S(1)} %embed.1), channel_id=1, source_target_pairs={{0,18},{1,13},{2,16},{3,15},{4,22},{5,9},{6,20},{7,11},{8,26},{9,5... | collective-permute-start | bytes 221192 | tf_op jit(solution)/shard_map/ppermute | solution.py:35
  6.4 0.5 %collective-permute-start.3 = (bf16[32,1152]{1,0:T(8,128)(2,1)S(1)}, bf16[32,1152]{1,0:T(8,128)(2,1)S(1)}, u32[]{:S(2)}, u32[]{:S(2)}) collective-permute-start(bf16[32,1152]{1,0:T(8,128)(2,1)S(1)} %embed.1), channel_id=1, source_target_pairs={{0,2},{1,5},{2,0},{3,7},{4,6},{5,1},{6,4},{7,3},{8,10},{9,13},{10,... | collective-permute-start | bytes 221192 | tf_op jit(solution)/shard_map/ppermute | solution.py:35
  6.9 0.1 collective-permute-start.4
  8.3 0.1 embed_other.1
  8.5 0.3 %collective-permute-done.2 = bf16[32,1152]{1,0:T(8,128)(2,1)S(1)} collective-permute-done((bf16[32,1152]{1,0:T(8,128)(2,1)S(1)}, bf16[32,1152]{1,0:T(8,128)(2,1)S(1)}, u32[]{:S(2)}, u32[]{:S(2)}) %collective-permute-start.2) | collective-permute-done | bytes 73760 | tf_op jit(solution)/shard_map/ppermute | solution.py:35
  8.7 0.8 %collective-permute-start.5 = (bf16[32,1152]{1,0:T(8,128)(2,1)S(1)}, bf16[32,1152]{1,0:T(8,128)(2,1)S(1)}, u32[]{:S(2)}, u32[]{:S(2)}) collective-permute-start(bf16[32,1152]{1,0:T(8,128)(2,1)S(1)} %collective-permute-done.2), channel_id=1, source_target_pairs={{0,1},{1,0},{2,3},{3,2},{4,5},{5,4},{6,7},{7,6},{8,9},{9,8},{10,11... | collective-permute-start | bytes 221192 | tf_op jit(solution)/shard_map/ppermute | solution.py:35
  9.5 1.3 %collective-permute-done.3 = bf16[32,1152]{1,0:T(8,128)(2,1)S(1)} collective-permute-done((bf16[32,1152]{1,0:T(8,128)(2,1)S(1)}, bf16[32,1152]{1,0:T(8,128)(2,1)S(1)}, u32[]{:S(2)}, u32[]{:S(2)}) %collective-permute-start.3) | collective-permute-done | bytes 73760 | tf_op jit(solution)/shard_map/ppermute | solution.py:35
  10.7 0.4 %collective-permute-start.6 = (bf16[32,1152]{1,0:T(8,128)(2,1)S(1)}, bf16[32,1152]{1,0:T(8,128)(2,1)S(1)}, u32[]{:S(2)}, u32[]{:S(2)}) collective-permute-start(bf16[32,1152]{1,0:T(8,128)(2,1)S(1)} %collective-permute-done.3), channel_id=1, source_target_pairs={{0,1},{1,0},{2,3},{3,2},{4,5},{5,4},{6,7},{7,6},{8,9},{9,8},{10,11... | collective-permute-start | bytes 221192 | tf_op jit(solution)/shard_map/ppermute | solution.py:35
  11.1 0.1 collective-permute-done.4
  11.2 0.5 %collective-permute-start.7 = (bf16[32,1152]{1,0:T(8,128)(2,1)S(1)}, bf16[32,1152]{1,0:T(8,128)(2,1)S(1)}, u32[]{:S(2)}, u32[]{:S(2)}) collective-permute-start(bf16[32,1152]{1,0:T(8,128)(2,1)S(1)} %collective-permute-done.4), channel_id=1, source_target_pairs={{0,1},{1,0},{2,3},{3,2},{4,5},{5,4},{6,7},{7,6},{8,9},{9,8},{10,11... | collective-permute-start | bytes 221192 | tf_op jit(solution)/shard_map/ppermute | solution.py:35
  11.7 0.0 collective-permute-done.5
  11.7 0.3 %collective-permute-done.6 = bf16[32,1152]{1,0:T(8,128)(2,1)S(1)} collective-permute-done((bf16[32,1152]{1,0:T(8,128)(2,1)S(1)}, bf16[32,1152]{1,0:T(8,128)(2,1)S(1)}, u32[]{:S(2)}, u32[]{:S(2)}) %collective-permute-start.6) | collective-permute-done | bytes 73760 | tf_op jit(solution)/shard_map/ppermute | solution.py:35
  12.0 0.6 %collective-permute-done.7 = bf16[32,1152]{1,0:T(8,128)(2,1)S(1)} collective-permute-done((bf16[32,1152]{1,0:T(8,128)(2,1)S(1)}, bf16[32,1152]{1,0:T(8,128)(2,1)S(1)}, u32[]{:S(2)}, u32[]{:S(2)}) %collective-permute-start.7) | collective-permute-done | bytes 73760 | tf_op jit(solution)/shard_map/ppermute | solution.py:35
  12.6 0.5 %tile.1 = (f32[296,128]{1,0:T(8,128)S(1)}, f32[296,128]{1,0:T(8,128)S(1)}, f32[296,128]{1,0:T(8,128)S(1)}, f32[296,128]{1,0:T(8,128)S(1)}) custom-call(f32[1]{0:T(128)} %bitcast.2.scale_ref, f32[1]{0:T(128)} %bitcast.3.shift_ref, bf16[128,1152]{1,0:T(8,128)(2,1)S(1)} %pad_maximum_fusion.mine, bf16[128,1152]{1,0:T(8,128)(2,1)S(1)} %pad_maximum_fusion.1.other), custom_call_target="tpu_custom_call" | custom-call | tf_op jit(solution)/shard_map/tile/pallas_call | solution.py:161
  13.2 2.5 %collective-permute-start.10 = (f16[296,128]{1,0:T(8,128)(2,1)S(1)}, f16[296,128]{1,0:T(8,128)(2,1)S(1)}, u32[]{:S(2)}, u32[]{:S(2)}) collective-permute-start(f16[296,128]{1,0:T(8,128)(2,1)S(1)} %multiply_convert_fusion), channel_id=1, source_target_pairs={{0,18},{1,13},{2,16},{3,15},{4,22},{5,9},{6,20},{7,11},{8,26},{9,5... | collective-permute-start | bytes 227336 | tf_op jit(solution)/shard_map/ppermute | solution.py:35
  15.7 0.6 %collective-permute-start.8 = (f16[296,128]{1,0:T(8,128)(2,1)S(1)}, f16[296,128]{1,0:T(8,128)(2,1)S(1)}, u32[]{:S(2)}, u32[]{:S(2)}) collective-permute-start(f16[296,128]{1,0:T(8,128)(2,1)S(1)} %multiply_convert_fusion.2), channel_id=1, source_target_pairs={{0,2},{1,5},{2,0},{3,7},{4,6},{5,1},{6,4},{7,3},{8,10},{9,13},{10,... | collective-permute-start | bytes 227336 | tf_op jit(solution)/shard_map/ppermute | solution.py:35
  16.3 0.6 %collective-permute-start.9 = (f16[296,128]{1,0:T(8,128)(2,1)S(1)}, f16[296,128]{1,0:T(8,128)(2,1)S(1)}, u32[]{:S(2)}, u32[]{:S(2)}) collective-permute-start(f16[296,128]{1,0:T(8,128)(2,1)S(1)} %multiply_convert_fusion.1), channel_id=1, source_target_pairs={{0,16},{1,9},{2,18},{3,11},{4,20},{5,13},{6,22},{7,15},{8,24},{9,1... | collective-permute-start | bytes 227336 | tf_op jit(solution)/shard_map/ppermute | solution.py:35
  16.9 1.6 %collective-permute-done.10 = f16[296,128]{1,0:T(8,128)(2,1)S(1)} collective-permute-done((f16[296,128]{1,0:T(8,128)(2,1)S(1)}, f16[296,128]{1,0:T(8,128)(2,1)S(1)}, u32[]{:S(2)}, u32[]{:S(2)}) %collective-permute-start.10) | collective-permute-done | bytes 75808 | tf_op jit(solution)/shard_map/ppermute | solution.py:35
  18.6 1.6 %collective-permute-done.8 = f16[296,128]{1,0:T(8,128)(2,1)S(1)} collective-permute-done((f16[296,128]{1,0:T(8,128)(2,1)S(1)}, f16[296,128]{1,0:T(8,128)(2,1)S(1)}, u32[]{:S(2)}, u32[]{:S(2)}) %collective-permute-start.8) | collective-permute-done | bytes 75808 | tf_op jit(solution)/shard_map/ppermute | solution.py:35
  20.2 0.6 %collective-permute-done.9 = f16[296,128]{1,0:T(8,128)(2,1)S(1)} collective-permute-done((f16[296,128]{1,0:T(8,128)(2,1)S(1)}, f16[296,128]{1,0:T(8,128)(2,1)S(1)}, u32[]{:S(2)}, u32[]{:S(2)}) %collective-permute-start.9) | collective-permute-done | bytes 75808 | tf_op jit(solution)/shard_map/ppermute | solution.py:35
  20.8 0.1 multiply_add_fusion
  20.9 0.0 copy-start
  20.9 0.2 %collective-permute-start.11 = (f32[152,128]{1,0:T(8,128)S(1)}, f32[152,128]{1,0:T(8,128)S(1)}, u32[]{:S(2)}, u32[]{:S(2)}) collective-permute-start(f32[152,128]{1,0:T(8,128)S(1)} %get-tuple-element.13), channel_id=1, source_target_pairs={{0,1},{1,0},{2,3},{3,2},{4,5},{5,4},{6,7},{7,6},{8,9},{9,8},{10,11... | collective-permute-start | bytes 233480 | tf_op jit(solution)/shard_map/ppermute | solution.py:35
  21.2 1.1 %collective-permute-done.11.came = f32[152,128]{1,0:T(8,128)S(1)} collective-permute-done((f32[152,128]{1,0:T(8,128)S(1)}, f32[152,128]{1,0:T(8,128)S(1)}, u32[]{:S(2)}, u32[]{:S(2)}) %collective-permute-start.11) | collective-permute-done | bytes 77856 | tf_op jit(solution)/shard_map/ppermute | solution.py:35
  22.2 0.0 copy-done
  22.2 0.9 %finish.1 = (f32[16]{0:T(128)}, f32[16,1152]{1,0:T(8,128)}, f32[16,1152]{1,0:T(8,128)}) custom-call(bf16[16,1152]{1,0:T(8,128)(2,1)S(1)} %copy-done, bf16[16,1152]{1,0:T(8,128)(2,1)S(1)} %copy-done.1, f32[152,128]{1,0:T(8,128)S(1)} %get-tuple-element.14.kept, f32[152,128]{1,0:T(8,128)S(1)} %collective-permute-done.11.came), custom_call_target="tpu_custom_call" | custom-call | tf_op jit(solution)/shard_map/finish/pallas_call | solution.py:180
  (9 shorter events, 0.1 us)
Async XLA Ops:
  0.6 1.4 %copy-start.1 = (bf16[16,1152]{1,0:T(8,128)(2,1)S(1)}, bf16[16,1152]{1,0:T(8,128)(2,1)}, u32[]{:S(2)}) copy-start(bf16[16,1152]{1,0:T(8,128)(2,1)} %texts.1) | copy-start | bytes 110596
  0.6 1.6 %collective-permute-start = (bf16[16,1152]{1,0:T(8,128)(2,1)}, bf16[16,1152]{1,0:T(8,128)(2,1)S(1)}, u32[]{:S(2)}, u32[]{:S(2)}) collective-permute-start(bf16[16,1152]{1,0:T(8,128)(2,1)} %images.1), channel_id=1, source_target_pairs={{0,1},{1,0},{2,3},{3,2},{4,5},{5,4},{6,7},{7,6},{8,9},{9,8},{10,11... | collective-permute-start | bytes 110600 | tf_op jit(solution)/shard_map/ppermute | solution.py:35
  1.2 1.4 %collective-permute-start.1 = (bf16[16,1152]{1,0:T(8,128)(2,1)}, bf16[16,1152]{1,0:T(8,128)(2,1)S(1)}, u32[]{:S(2)}, u32[]{:S(2)}) collective-permute-start(bf16[16,1152]{1,0:T(8,128)(2,1)} %texts.1), channel_id=1, source_target_pairs={{0,1},{1,0},{2,3},{3,2},{4,5},{5,4},{6,7},{7,6},{8,9},{9,8},{10,11... | collective-permute-start | bytes 110600 | tf_op jit(solution)/shard_map/ppermute | solution.py:35
  2.7 6.0 %collective-permute-start.2 = (bf16[32,1152]{1,0:T(8,128)(2,1)S(1)}, bf16[32,1152]{1,0:T(8,128)(2,1)S(1)}, u32[]{:S(2)}, u32[]{:S(2)}) collective-permute-start(bf16[32,1152]{1,0:T(8,128)(2,1)S(1)} %embed.1), channel_id=1, source_target_pairs={{0,18},{1,13},{2,16},{3,15},{4,22},{5,9},{6,20},{7,11},{8,26},{9,5... | collective-permute-start | bytes 221192 | tf_op jit(solution)/shard_map/ppermute | solution.py:35
  6.4 4.4 %collective-permute-start.3 = (bf16[32,1152]{1,0:T(8,128)(2,1)S(1)}, bf16[32,1152]{1,0:T(8,128)(2,1)S(1)}, u32[]{:S(2)}, u32[]{:S(2)}) collective-permute-start(bf16[32,1152]{1,0:T(8,128)(2,1)S(1)} %embed.1), channel_id=1, source_target_pairs={{0,2},{1,5},{2,0},{3,7},{4,6},{5,1},{6,4},{7,3},{8,10},{9,13},{10,... | collective-permute-start | bytes 221192 | tf_op jit(solution)/shard_map/ppermute | solution.py:35
  6.9 4.4 %collective-permute-start.4 = (bf16[32,1152]{1,0:T(8,128)(2,1)S(1)}, bf16[32,1152]{1,0:T(8,128)(2,1)S(1)}, u32[]{:S(2)}, u32[]{:S(2)}) collective-permute-start(bf16[32,1152]{1,0:T(8,128)(2,1)S(1)} %embed.1), channel_id=1, source_target_pairs={{0,16},{1,9},{2,18},{3,11},{4,20},{5,13},{6,22},{7,15},{8,24},{9,1... | collective-permute-start | bytes 221192 | tf_op jit(solution)/shard_map/ppermute | solution.py:35
  8.7 3.0 %collective-permute-start.5 = (bf16[32,1152]{1,0:T(8,128)(2,1)S(1)}, bf16[32,1152]{1,0:T(8,128)(2,1)S(1)}, u32[]{:S(2)}, u32[]{:S(2)}) collective-permute-start(bf16[32,1152]{1,0:T(8,128)(2,1)S(1)} %collective-permute-done.2), channel_id=1, source_target_pairs={{0,1},{1,0},{2,3},{3,2},{4,5},{5,4},{6,7},{7,6},{8,9},{9,8},{10,11... | collective-permute-start | bytes 221192 | tf_op jit(solution)/shard_map/ppermute | solution.py:35
  10.7 1.3 %collective-permute-start.6 = (bf16[32,1152]{1,0:T(8,128)(2,1)S(1)}, bf16[32,1152]{1,0:T(8,128)(2,1)S(1)}, u32[]{:S(2)}, u32[]{:S(2)}) collective-permute-start(bf16[32,1152]{1,0:T(8,128)(2,1)S(1)} %collective-permute-done.3), channel_id=1, source_target_pairs={{0,1},{1,0},{2,3},{3,2},{4,5},{5,4},{6,7},{7,6},{8,9},{9,8},{10,11... | collective-permute-start | bytes 221192 | tf_op jit(solution)/shard_map/ppermute | solution.py:35
  11.2 1.4 %collective-permute-start.7 = (bf16[32,1152]{1,0:T(8,128)(2,1)S(1)}, bf16[32,1152]{1,0:T(8,128)(2,1)S(1)}, u32[]{:S(2)}, u32[]{:S(2)}) collective-permute-start(bf16[32,1152]{1,0:T(8,128)(2,1)S(1)} %collective-permute-done.4), channel_id=1, source_target_pairs={{0,1},{1,0},{2,3},{3,2},{4,5},{5,4},{6,7},{7,6},{8,9},{9,8},{10,11... | collective-permute-start | bytes 221192 | tf_op jit(solution)/shard_map/ppermute | solution.py:35
  13.2 5.3 %collective-permute-start.10 = (f16[296,128]{1,0:T(8,128)(2,1)S(1)}, f16[296,128]{1,0:T(8,128)(2,1)S(1)}, u32[]{:S(2)}, u32[]{:S(2)}) collective-permute-start(f16[296,128]{1,0:T(8,128)(2,1)S(1)} %multiply_convert_fusion), channel_id=1, source_target_pairs={{0,18},{1,13},{2,16},{3,15},{4,22},{5,9},{6,20},{7,11},{8,26},{9,5... | collective-permute-start | bytes 227336 | tf_op jit(solution)/shard_map/ppermute | solution.py:35
  15.7 4.4 %collective-permute-start.8 = (f16[296,128]{1,0:T(8,128)(2,1)S(1)}, f16[296,128]{1,0:T(8,128)(2,1)S(1)}, u32[]{:S(2)}, u32[]{:S(2)}) collective-permute-start(f16[296,128]{1,0:T(8,128)(2,1)S(1)} %multiply_convert_fusion.2), channel_id=1, source_target_pairs={{0,2},{1,5},{2,0},{3,7},{4,6},{5,1},{6,4},{7,3},{8,10},{9,13},{10,... | collective-permute-start | bytes 227336 | tf_op jit(solution)/shard_map/ppermute | solution.py:35
  16.3 4.4 %collective-permute-start.9 = (f16[296,128]{1,0:T(8,128)(2,1)S(1)}, f16[296,128]{1,0:T(8,128)(2,1)S(1)}, u32[]{:S(2)}, u32[]{:S(2)}) collective-permute-start(f16[296,128]{1,0:T(8,128)(2,1)S(1)} %multiply_convert_fusion.1), channel_id=1, source_target_pairs={{0,16},{1,9},{2,18},{3,11},{4,20},{5,13},{6,22},{7,15},{8,24},{9,1... | collective-permute-start | bytes 227336 | tf_op jit(solution)/shard_map/ppermute | solution.py:35
  20.9 1.4 %copy-start = (bf16[16,1152]{1,0:T(8,128)(2,1)S(1)}, bf16[16,1152]{1,0:T(8,128)(2,1)}, u32[]{:S(2)}) copy-start(bf16[16,1152]{1,0:T(8,128)(2,1)} %images.1) | copy-start | bytes 110596
  20.9 1.3 %collective-permute-start.11 = (f32[152,128]{1,0:T(8,128)S(1)}, f32[152,128]{1,0:T(8,128)S(1)}, u32[]{:S(2)}, u32[]{:S(2)}) collective-permute-start(f32[152,128]{1,0:T(8,128)S(1)} %get-tuple-element.13), channel_id=1, source_target_pairs={{0,1},{1,0},{2,3},{3,2},{4,5},{5,4},{6,7},{7,6},{8,9},{9,8},{10,11... | collective-permute-start | bytes 233480 | tf_op jit(solution)/shard_map/ppermute | solution.py:35

commit v5 on v3

v5 whole, which is shorter than its diff:
```python
import functools

import jax
import jax.numpy as jnp
from jax import lax
from jax.experimental import pallas as pl
from jax.experimental.pallas import tpu as pltpu
from jax.sharding import PartitionSpec as P

AXES = ("blk", "grp")
LANES = 128
SCALE_TOP = 16.0
FLOAT16_TOP = 65504.0
VMEM_BYTES = 24 * 1024 * 1024


def spread(value, bits):
    return sum(bit for place, bit in enumerate(bits) if value >> place & 1)


def plan(blocks, groups):
    bits = [1 << place for place in range((blocks * groups).bit_length() - 1)][1:]
    half = len(bits) // 2
    top = [bit for bit in bits if bit >= groups]
    low = [bit for bit in bits if bit < groups]
    need = half - len(top)
    image_bits = low[:need] + top
    text_bits = low[need:]
    last = (1 << half) - 1
    return [(spread(k, image_bits), spread(k, text_bits)) for k in [*range(last - 1, 0, -1), last]]


def permuted(value, devices, image_step, text_step):
    pairs = [(d, d ^ (text_step if d & 1 else image_step)) for d in range(devices)]
    return lax.ppermute(value, AXES, pairs)


def first_core():
    return lax.axis_index("grp") % 2 == 0


def message_lift(count):
    lift = 1.0
    while lift * 2 * count * SCALE_TOP < FLOAT16_TOP:
        lift *= 2
    return lift


def units(values):
    floats = values.astype(jnp.float32)
    norms = jnp.sqrt(jnp.sum(floats * floats, 1, keepdims=True) + 1e-06)
    return floats / norms, norms


def place(out, raw, near):
    rows = raw.shape[0]
    out[:rows, :] = units(raw)[0].astype(jnp.bfloat16)
    out[rows:, :] = units(near[...])[0].astype(jnp.bfloat16)


def by_core(takes_images, own, images_near, texts_near, out):
    rows = images_near.shape[0]

    @pl.when(takes_images)
    def _():
        place(out, own[:rows, :], images_near)

    @pl.when(jnp.logical_not(takes_images))
    def _():
        place(out, own[rows:, :], texts_near)


def embed_kernel(own, images_near, texts_near, chip):
    by_core(first_core(), own, images_near, texts_near, chip)


def embed_other_kernel(own, images_near, texts_near, chip, unit_out, norm_out):
    by_core(jnp.logical_not(first_core()), own, images_near, texts_near, chip)
    unit, norm = units(own[...])
    unit_out[...] = unit
    norm_out[...] = jnp.broadcast_to(norm, norm_out.shape)


def tile_kernel(rows, scale_ref, shift_ref, mine, other, *outs):
    scale = scale_ref[0]
    shift = shift_ref[0]
    own = mine[...]
    far = other[...]
    count = own.shape[0]
    size = 2 * rows
    nt = (((1,), (1,)), ((), ()))
    row = lax.broadcasted_iota(jnp.int32, (count, count), 0)
    column = lax.broadcasted_iota(jnp.int32, (count, count), 1)
    hit = jnp.logical_and(row == column, row < size)
    label = hit.astype(jnp.float32)
    logit = scale * lax.dot_general(own, far, nt, preferred_element_type=jnp.float32) + shift
    coef = ((jax.nn.sigmoid(logit) - label) * scale).astype(jnp.bfloat16)
    grad = jnp.dot(coef, far, preferred_element_type=jnp.float32)
    signed = logit * (1.0 - 2.0 * label)
    soft = jnp.maximum(signed, 0.0) + jnp.log1p(jnp.exp(-jnp.abs(signed)))
    loss = jnp.sum(soft.T, 0, keepdims=True)
    chunks = own.shape[1] // LANES
    half = chunks * rows + 8
    for slot, out in enumerate(outs):
        top = slot * size
        part = loss[:, top // LANES * LANES : top // LANES * LANES + LANES]
        part = jnp.broadcast_to(part, (8, LANES))
        if top % LANES:
            part = pltpu.roll(part, LANES - top % LANES, 1)
        for side in range(2):
            for chunk in range(chunks):
                at = side * half + chunk * rows
                out[at : at + rows, :] = grad[
                    top + side * rows : top + (side + 1) * rows, chunk * LANES : (chunk + 1) * LANES
                ]
            out[(side + 1) * half - 8 : (side + 1) * half, :] = part


def finish_kernel(total, unit, norm, kept, came, loss_out, image_out, text_out):
    rows, width = image_out.shape
    chunks = width // LANES
    at = chunks * rows

    def back(role, grads):
        own = unit[role * rows : (role + 1) * rows, :]
        grad = jnp.concatenate(
            [grads[chunk * rows : (chunk + 1) * rows, :] for chunk in range(chunks)], 1
        )
        flat = grad - own * jnp.sum(own * grad, 1, keepdims=True)
        return flat / norm[role * rows : (role + 1) * rows, :1]

    first = first_core()

    @pl.when(first)
    def _():
        image_out[...] = back(0, kept)
        text_out[...] = back(1, came)
        loss_out[...] = kept[at, :rows] / total

    @pl.when(jnp.logical_not(first))
    def _():
        image_out[...] = back(0, came)
        text_out[...] = back(1, kept)
        loss_out[...] = pltpu.roll(came[at:, :], LANES - rows, 1)[0, :rows] / total


def vmem(count):
    return [pl.BlockSpec(memory_space=pltpu.VMEM)] * count


def local(images, texts, scale, shift, blocks, groups):
    rows, width = images.shape
    devices = blocks * groups
    params = pltpu.CompilerParams(vmem_limit_bytes=VMEM_BYTES)
    steps = plan(blocks, groups)
    chunks = width // LANES
    images_near = permuted(images, devices, 1, 1)
    texts_near = permuted(texts, devices, 1, 1)
    own = jnp.concatenate([images, texts], 0)
    raws = (own, images_near, texts_near)
    piece = jax.ShapeDtypeStruct((2 * rows, width), jnp.bfloat16)
    chip = pl.pallas_call(
        embed_kernel,
        out_shape=piece,
        in_specs=vmem(3),
        out_specs=vmem(1)[0],
        compiler_params=params,
        name="embed",
    )(*raws)
    chip_other, unit, norm = pl.pallas_call(
        embed_other_kernel,
        out_shape=(
            piece,
            jax.ShapeDtypeStruct((2 * rows, width), jnp.float32),
            jax.ShapeDtypeStruct((2 * rows, LANES), jnp.float32),
        ),
        in_specs=vmem(3),
        out_specs=tuple(vmem(3)),
        compiler_params=params,
        name="embed_other",
    )(*raws)
    gathered = [permuted(chip, devices, a, b) for a, b in steps]
    slots = len(steps) + 1
    mine = jnp.concatenate([chip] + gathered, 0)
    other = jnp.concatenate([chip_other] + [permuted(part, devices, 1, 1) for part in gathered], 0)
    half = chunks * rows + 8
    message = jax.ShapeDtypeStruct((2 * half, LANES), jnp.float32)
    parts = pl.pallas_call(
        functools.partial(tile_kernel, rows),
        out_shape=[message] * slots,
        in_specs=[pl.BlockSpec(memory_space=pltpu.SMEM)] * 2 + vmem(2),
        out_specs=vmem(slots),
        compiler_params=params,
        name="tile",
    )(scale.reshape(1), shift.reshape(1), mine, other)
    lift = message_lift(2 * rows * slots)
    whole = parts[0]
    for part, (a, b) in zip(parts[1:], steps):
        sent = (part * lift).astype(jnp.float16)
        whole = whole + permuted(sent, devices, a, b).astype(jnp.float32) * (1.0 / lift)
    kept = whole[:half]
    came = permuted(whole[half:], devices, 1, 1)
    return pl.pallas_call(
        functools.partial(finish_kernel, devices * rows),
        out_shape=(
            jax.ShapeDtypeStruct((rows,), jnp.float32),
            jax.ShapeDtypeStruct((rows, width), jnp.float32),
            jax.ShapeDtypeStruct((rows, width), jnp.float32),
        ),
        in_specs=vmem(4),
        out_specs=tuple(vmem(3)),
        compiler_params=params,
        name="finish",
    )(unit, norm, kept, came)


def solution(mesh):
    in_specs = (P(AXES, None), P(AXES, None), P(), P())
    out_specs = (P(AXES), P(AXES, None), P(AXES, None))
    step = functools.partial(local, blocks=mesh.shape["blk"], groups=mesh.shape["grp"])
    return jax.shard_map(step, mesh=mesh, in_specs=in_specs, out_specs=out_specs, check_vma=False)
```

time: 23.7 us -> 23.1 us (0.975)
  waiting for transfers between devices: 9.72 us -> 7.84 us
  starting transfers between devices: 9.22 us -> 10.4 us
  local copies, waits for them, and re-layouts: 0.02 us -> 0.8 us
  other arithmetic: 0.94 us -> 0.16 us
    ppermute x10 -> x12, waiting for transfers between devices: 9.72 us -> 7.84 us  [permuted(): return lax.ppermute(value, AXES, pairs)]
    ppermute x10 -> x12, starting transfers between devices: 9.22 us -> 10.4 us  [permuted(): return lax.ppermute(value, AXES, pairs)]
    select_n x2 -> x0, other arithmetic: 0.79 us -> none  [the longest x1 0.78 us: local(): jnp.where(first, images, texts)]
    unnamed x4 -> x3, local copies, waits for them, and re-layouts: 0.01 us -> 0.77 us
    pallas_call x1 -> x2, Pallas kernels: 0.12 us -> 0.36 us  [the longest x1 0.25 us: local(): pl.pallas_call(embed_other_kernel, out_shape=(piece, jax.ShapeDtypeStruct...]
  transfers between devices with their start and end apart: 10 -> 12, of which waited for: 9 -> 11; matrix products, arithmetic and copies ran while one was open for 3% -> 4% of each run, Pallas kernels for 0% -> 1%
where the time goes in v5:
time: 23.1 us; the launch traced here: 22.9 us
  starting transfers between devices  10.4 us (45%)
  waiting for transfers between devices  7.84 us (34%)
  between operations  2.02 us (9%)
  Pallas kernels  1.68 us (7%)
  local copies, waits for them, and re-layouts  0.8 us (3%)
    ppermute x12, starting transfers between devices, permuted(): return lax.ppermute(value, AXES, pairs)  10.4 us
    ppermute x12, waiting for transfers between devices, permuted(): return lax.ppermute(value, AXES, pairs)  7.84 us
    pallas_call x1, Pallas kernels, local(): pl.pallas_call(functools.partial(finish_kernel, devices * rows), out_shap...  0.78 us
    unnamed x3, local copies, waits for them, and re-layouts  0.77 us
    pallas_call x1, Pallas kernels, local(): pl.pallas_call(functools.partial(tile_kernel, rows), out_shape=[message]...  0.54 us
  transfers between devices with their start and end apart: 12, of which 11 were waited for; matrix products, arithmetic and copies ran while one was open for 4% of the time, Pallas kernels for 1%

profile of v5, /device:TPU:0, one launch (start us, length us, event | category | flops | bytes accessed | tf_op | source)
XLA Modules:
  0.0 22.9 jit_solution(4627858044365743218)
XLA Ops:
  0.6 0.0 copy-start
  0.6 0.5 %collective-permute-start = (bf16[16,1152]{1,0:T(8,128)(2,1)}, bf16[16,1152]{1,0:T(8,128)(2,1)S(1)}, u32[]{:S(2)}, u32[]{:S(2)}) collective-permute-start(bf16[16,1152]{1,0:T(8,128)(2,1)} %param.4), channel_id=1, source_target_pairs={{0,1},{1,0},{2,3},{3,2},{4,5},{5,4},{6,7},{7,6},{8,9},{9,8},{10,11... | collective-permute-start | bytes 110600 | tf_op jit(solution)/shard_map/ppermute | solution.py:35
  1.2 0.1 collective-permute-start.1
  1.2 0.8 %constant_dynamic-update-slice_fusion.1 = bf16[32,1152]{1,0:T(8,128)(2,1)S(1)} fusion(bf16[16,1152]{1,0:T(8,128)(2,1)} %param.4), kind=kLoop, calls=%fused_computation.7 | loop fusion | bytes 73728
  2.0 0.0 copy-done
  2.0 0.2 collective-permute-done.images_near
  2.2 0.3 %collective-permute-done.1.texts_near = bf16[16,1152]{1,0:T(8,128)(2,1)S(1)} collective-permute-done((bf16[16,1152]{1,0:T(8,128)(2,1)}, bf16[16,1152]{1,0:T(8,128)(2,1)S(1)}, u32[]{:S(2)}, u32[]{:S(2)}) %collective-permute-start.1) | collective-permute-done | bytes 36896 | tf_op jit(solution)/shard_map/ppermute | solution.py:35
  2.6 0.1 embed.1
  2.7 3.7 %collective-permute-start.4 = (bf16[32,1152]{1,0:T(8,128)(2,1)S(1)}, bf16[32,1152]{1,0:T(8,128)(2,1)S(1)}, u32[]{:S(2)}, u32[]{:S(2)}) collective-permute-start(bf16[32,1152]{1,0:T(8,128)(2,1)S(1)} %embed.1), channel_id=1, source_target_pairs={{0,18},{1,13},{2,16},{3,15},{4,22},{5,9},{6,20},{7,11},{8,26},{9,5... | collective-permute-start | bytes 221192 | tf_op jit(solution)/shard_map/ppermute | solution.py:35
  6.4 0.5 %collective-permute-start.3 = (bf16[32,1152]{1,0:T(8,128)(2,1)S(1)}, bf16[32,1152]{1,0:T(8,128)(2,1)S(1)}, u32[]{:S(2)}, u32[]{:S(2)}) collective-permute-start(bf16[32,1152]{1,0:T(8,128)(2,1)S(1)} %embed.1), channel_id=1, source_target_pairs={{0,2},{1,5},{2,0},{3,7},{4,6},{5,1},{6,4},{7,3},{8,10},{9,13},{10,... | collective-permute-start | bytes 221192 | tf_op jit(solution)/shard_map/ppermute | solution.py:35
  6.9 0.1 collective-permute-start.2
  8.3 0.2 %embed_other.1 = (bf16[32,1152]{1,0:T(8,128)(2,1)S(1)}, f32[32,1152]{1,0:T(8,128)S(1)}, f32[32,128]{1,0:T(8,128)S(1)}) custom-call(bf16[32,1152]{1,0:T(8,128)(2,1)S(1)} %constant_dynamic-update-slice_fusion.own, bf16[16,1152]{1,0:T(8,128)(2,1)S(1)} %collective-permute-done.images_near, bf16[16,1152]{1,0:T(8,128)(2,1)S(1)} %collective-permute-done.1.texts_near), custom_call_target="tpu_custom_call" | custom-call | tf_op jit(solution)/shard_map/embed_other/pallas_call | solution.py:170
  8.6 0.1 collective-permute-done.4
  8.7 0.9 %collective-permute-start.7 = (bf16[32,1152]{1,0:T(8,128)(2,1)S(1)}, bf16[32,1152]{1,0:T(8,128)(2,1)S(1)}, u32[]{:S(2)}, u32[]{:S(2)}) collective-permute-start(bf16[32,1152]{1,0:T(8,128)(2,1)S(1)} %collective-permute-done.4), channel_id=1, source_target_pairs={{0,1},{1,0},{2,3},{3,2},{4,5},{5,4},{6,7},{7,6},{8,9},{9,8},{10,11... | collective-permute-start | bytes 221192 | tf_op jit(solution)/shard_map/ppermute | solution.py:35
  9.6 1.1 %collective-permute-done.3 = bf16[32,1152]{1,0:T(8,128)(2,1)S(1)} collective-permute-done((bf16[32,1152]{1,0:T(8,128)(2,1)S(1)}, bf16[32,1152]{1,0:T(8,128)(2,1)S(1)}, u32[]{:S(2)}, u32[]{:S(2)}) %collective-permute-start.3) | collective-permute-done | bytes 73760 | tf_op jit(solution)/shard_map/ppermute | solution.py:35
  10.7 0.4 %collective-permute-start.6 = (bf16[32,1152]{1,0:T(8,128)(2,1)S(1)}, bf16[32,1152]{1,0:T(8,128)(2,1)S(1)}, u32[]{:S(2)}, u32[]{:S(2)}) collective-permute-start(bf16[32,1152]{1,0:T(8,128)(2,1)S(1)} %collective-permute-done.3), channel_id=1, source_target_pairs={{0,1},{1,0},{2,3},{3,2},{4,5},{5,4},{6,7},{7,6},{8,9},{9,8},{10,11... | collective-permute-start | bytes 221192 | tf_op jit(solution)/shard_map/ppermute | solution.py:35
  11.1 0.1 collective-permute-done.2
  11.2 0.5 %collective-permute-start.5 = (bf16[32,1152]{1,0:T(8,128)(2,1)S(1)}, bf16[32,1152]{1,0:T(8,128)(2,1)S(1)}, u32[]{:S(2)}, u32[]{:S(2)}) collective-permute-start(bf16[32,1152]{1,0:T(8,128)(2,1)S(1)} %collective-permute-done.2), channel_id=1, source_target_pairs={{0,1},{1,0},{2,3},{3,2},{4,5},{5,4},{6,7},{7,6},{8,9},{9,8},{10,11... | collective-permute-start | bytes 221192 | tf_op jit(solution)/shard_map/ppermute | solution.py:35
  11.7 0.0 collective-permute-done.7
  11.7 0.3 %collective-permute-done.6 = bf16[32,1152]{1,0:T(8,128)(2,1)S(1)} collective-permute-done((bf16[32,1152]{1,0:T(8,128)(2,1)S(1)}, bf16[32,1152]{1,0:T(8,128)(2,1)S(1)}, u32[]{:S(2)}, u32[]{:S(2)}) %collective-permute-start.6) | collective-permute-done | bytes 73760 | tf_op jit(solution)/shard_map/ppermute | solution.py:35
  12.0 0.6 %collective-permute-done.5 = bf16[32,1152]{1,0:T(8,128)(2,1)S(1)} collective-permute-done((bf16[32,1152]{1,0:T(8,128)(2,1)S(1)}, bf16[32,1152]{1,0:T(8,128)(2,1)S(1)}, u32[]{:S(2)}, u32[]{:S(2)}) %collective-permute-start.5) | collective-permute-done | bytes 73760 | tf_op jit(solution)/shard_map/ppermute | solution.py:35
  12.6 0.5 %tile.1 = (f32[304,128]{1,0:T(8,128)S(1)}, f32[304,128]{1,0:T(8,128)S(1)}, f32[304,128]{1,0:T(8,128)S(1)}, f32[304,128]{1,0:T(8,128)S(1)}) custom-call(f32[1]{0:T(128)} %bitcast.2.scale_ref, f32[1]{0:T(128)} %bitcast.3.shift_ref, bf16[128,1152]{1,0:T(8,128)(2,1)S(1)} %pad_maximum_fusion.mine, bf16[128,1152]{1,0:T(8,128)(2,1)S(1)} %pad_maximum_fusion.1.other), custom_call_target="tpu_custom_call" | custom-call | tf_op jit(solution)/shard_map/tile/pallas_call | solution.py:188
  13.3 2.5 %collective-permute-start.10 = (f16[304,128]{1,0:T(8,128)(2,1)S(1)}, f16[304,128]{1,0:T(8,128)(2,1)S(1)}, u32[]{:S(2)}, u32[]{:S(2)}) collective-permute-start(f16[304,128]{1,0:T(8,128)(2,1)S(1)} %multiply_convert_fusion), channel_id=1, source_target_pairs={{0,18},{1,13},{2,16},{3,15},{4,22},{5,9},{6,20},{7,11},{8,26},{9,5... | collective-permute-start | bytes 233480 | tf_op jit(solution)/shard_map/ppermute | solution.py:35
  15.8 0.5 %collective-permute-start.9 = (f16[304,128]{1,0:T(8,128)(2,1)S(1)}, f16[304,128]{1,0:T(8,128)(2,1)S(1)}, u32[]{:S(2)}, u32[]{:S(2)}) collective-permute-start(f16[304,128]{1,0:T(8,128)(2,1)S(1)} %multiply_convert_fusion.1), channel_id=1, source_target_pairs={{0,2},{1,5},{2,0},{3,7},{4,6},{5,1},{6,4},{7,3},{8,10},{9,13},{10,... | collective-permute-start | bytes 233480 | tf_op jit(solution)/shard_map/ppermute | solution.py:35
  16.3 0.5 %collective-permute-start.8 = (f16[304,128]{1,0:T(8,128)(2,1)S(1)}, f16[304,128]{1,0:T(8,128)(2,1)S(1)}, u32[]{:S(2)}, u32[]{:S(2)}) collective-permute-start(f16[304,128]{1,0:T(8,128)(2,1)S(1)} %multiply_convert_fusion.2), channel_id=1, source_target_pairs={{0,16},{1,9},{2,18},{3,11},{4,20},{5,13},{6,22},{7,15},{8,24},{9,1... | collective-permute-start | bytes 233480 | tf_op jit(solution)/shard_map/ppermute | solution.py:35
  16.8 1.8 %collective-permute-done.10 = f16[304,128]{1,0:T(8,128)(2,1)S(1)} collective-permute-done((f16[304,128]{1,0:T(8,128)(2,1)S(1)}, f16[304,128]{1,0:T(8,128)(2,1)S(1)}, u32[]{:S(2)}, u32[]{:S(2)}) %collective-permute-start.10) | collective-permute-done | bytes 77856 | tf_op jit(solution)/shard_map/ppermute | solution.py:35
  18.6 1.5 %collective-permute-done.9 = f16[304,128]{1,0:T(8,128)(2,1)S(1)} collective-permute-done((f16[304,128]{1,0:T(8,128)(2,1)S(1)}, f16[304,128]{1,0:T(8,128)(2,1)S(1)}, u32[]{:S(2)}, u32[]{:S(2)}) %collective-permute-start.9) | collective-permute-done | bytes 77856 | tf_op jit(solution)/shard_map/ppermute | solution.py:35
  20.2 0.5 %collective-permute-done.8 = f16[304,128]{1,0:T(8,128)(2,1)S(1)} collective-permute-done((f16[304,128]{1,0:T(8,128)(2,1)S(1)}, f16[304,128]{1,0:T(8,128)(2,1)S(1)}, u32[]{:S(2)}, u32[]{:S(2)}) %collective-permute-start.8) | collective-permute-done | bytes 77856 | tf_op jit(solution)/shard_map/ppermute | solution.py:35
  20.7 0.1 multiply_add_fusion
  20.8 0.2 %collective-permute-start.11 = (f32[152,128]{1,0:T(8,128)S(1)}, f32[152,128]{1,0:T(8,128)S(1)}, u32[]{:S(2)}, u32[]{:S(2)}) collective-permute-start(f32[152,128]{1,0:T(8,128)S(1)} %get-tuple-element.17), channel_id=1, source_target_pairs={{0,1},{1,0},{2,3},{3,2},{4,5},{5,4},{6,7},{7,6},{8,9},{9,8},{10,11... | collective-permute-start | bytes 233480 | tf_op jit(solution)/shard_map/ppermute | solution.py:35
  21.0 1.1 %collective-permute-done.11.came = f32[152,128]{1,0:T(8,128)S(1)} collective-permute-done((f32[152,128]{1,0:T(8,128)S(1)}, f32[152,128]{1,0:T(8,128)S(1)}, u32[]{:S(2)}, u32[]{:S(2)}) %collective-permute-start.11) | collective-permute-done | bytes 77856 | tf_op jit(solution)/shard_map/ppermute | solution.py:35
  22.1 0.8 %finish.1 = (f32[16]{0:T(128)}, f32[16,1152]{1,0:T(8,128)}, f32[16,1152]{1,0:T(8,128)}) custom-call(f32[32,1152]{1,0:T(8,128)S(1)} %get-tuple-element.10.unit, f32[32,128]{1,0:T(8,128)S(1)} %get-tuple-element.11.norm, f32[152,128]{1,0:T(8,128)S(1)} %get-tuple-element.18.kept, f32[152,128]{1,0:T(8,128)S(1)} %collective-permute-done.11.came), custom_call_target="tpu_custom_call" | custom-call | tf_op jit(solution)/shard_map/finish/pallas_call | solution.py:203
  (7 shorter events, 0.1 us)
Async XLA Ops:
  0.6 1.4 %copy-start = (bf16[16,1152]{1,0:T(8,128)(2,1)S(1)}, bf16[16,1152]{1,0:T(8,128)(2,1)}, u32[]{:S(2)}) copy-start(bf16[16,1152]{1,0:T(8,128)(2,1)} %param.5) | copy-start | bytes 110596
  0.6 1.6 %collective-permute-start = (bf16[16,1152]{1,0:T(8,128)(2,1)}, bf16[16,1152]{1,0:T(8,128)(2,1)S(1)}, u32[]{:S(2)}, u32[]{:S(2)}) collective-permute-start(bf16[16,1152]{1,0:T(8,128)(2,1)} %param.4), channel_id=1, source_target_pairs={{0,1},{1,0},{2,3},{3,2},{4,5},{5,4},{6,7},{7,6},{8,9},{9,8},{10,11... | collective-permute-start | bytes 110600 | tf_op jit(solution)/shard_map/ppermute | solution.py:35
  1.2 1.4 %collective-permute-start.1 = (bf16[16,1152]{1,0:T(8,128)(2,1)}, bf16[16,1152]{1,0:T(8,128)(2,1)S(1)}, u32[]{:S(2)}, u32[]{:S(2)}) collective-permute-start(bf16[16,1152]{1,0:T(8,128)(2,1)} %param.5), channel_id=1, source_target_pairs={{0,1},{1,0},{2,3},{3,2},{4,5},{5,4},{6,7},{7,6},{8,9},{9,8},{10,11... | collective-permute-start | bytes 110600 | tf_op jit(solution)/shard_map/ppermute | solution.py:35
  2.7 6.0 %collective-permute-start.4 = (bf16[32,1152]{1,0:T(8,128)(2,1)S(1)}, bf16[32,1152]{1,0:T(8,128)(2,1)S(1)}, u32[]{:S(2)}, u32[]{:S(2)}) collective-permute-start(bf16[32,1152]{1,0:T(8,128)(2,1)S(1)} %embed.1), channel_id=1, source_target_pairs={{0,18},{1,13},{2,16},{3,15},{4,22},{5,9},{6,20},{7,11},{8,26},{9,5... | collective-permute-start | bytes 221192 | tf_op jit(solution)/shard_map/ppermute | solution.py:35
  6.4 4.4 %collective-permute-start.3 = (bf16[32,1152]{1,0:T(8,128)(2,1)S(1)}, bf16[32,1152]{1,0:T(8,128)(2,1)S(1)}, u32[]{:S(2)}, u32[]{:S(2)}) collective-permute-start(bf16[32,1152]{1,0:T(8,128)(2,1)S(1)} %embed.1), channel_id=1, source_target_pairs={{0,2},{1,5},{2,0},{3,7},{4,6},{5,1},{6,4},{7,3},{8,10},{9,13},{10,... | collective-permute-start | bytes 221192 | tf_op jit(solution)/shard_map/ppermute | solution.py:35
  6.9 4.4 %collective-permute-start.2 = (bf16[32,1152]{1,0:T(8,128)(2,1)S(1)}, bf16[32,1152]{1,0:T(8,128)(2,1)S(1)}, u32[]{:S(2)}, u32[]{:S(2)}) collective-permute-start(bf16[32,1152]{1,0:T(8,128)(2,1)S(1)} %embed.1), channel_id=1, source_target_pairs={{0,16},{1,9},{2,18},{3,11},{4,20},{5,13},{6,22},{7,15},{8,24},{9,1... | collective-permute-start | bytes 221192 | tf_op jit(solution)/shard_map/ppermute | solution.py:35
  8.7 3.0 %collective-permute-start.7 = (bf16[32,1152]{1,0:T(8,128)(2,1)S(1)}, bf16[32,1152]{1,0:T(8,128)(2,1)S(1)}, u32[]{:S(2)}, u32[]{:S(2)}) collective-permute-start(bf16[32,1152]{1,0:T(8,128)(2,1)S(1)} %collective-permute-done.4), channel_id=1, source_target_pairs={{0,1},{1,0},{2,3},{3,2},{4,5},{5,4},{6,7},{7,6},{8,9},{9,8},{10,11... | collective-permute-start | bytes 221192 | tf_op jit(solution)/shard_map/ppermute | solution.py:35
  10.7 1.3 %collective-permute-start.6 = (bf16[32,1152]{1,0:T(8,128)(2,1)S(1)}, bf16[32,1152]{1,0:T(8,128)(2,1)S(1)}, u32[]{:S(2)}, u32[]{:S(2)}) collective-permute-start(bf16[32,1152]{1,0:T(8,128)(2,1)S(1)} %collective-permute-done.3), channel_id=1, source_target_pairs={{0,1},{1,0},{2,3},{3,2},{4,5},{5,4},{6,7},{7,6},{8,9},{9,8},{10,11... | collective-permute-start | bytes 221192 | tf_op jit(solution)/shard_map/ppermute | solution.py:35
  11.2 1.4 %collective-permute-start.5 = (bf16[32,1152]{1,0:T(8,128)(2,1)S(1)}, bf16[32,1152]{1,0:T(8,128)(2,1)S(1)}, u32[]{:S(2)}, u32[]{:S(2)}) collective-permute-start(bf16[32,1152]{1,0:T(8,128)(2,1)S(1)} %collective-permute-done.2), channel_id=1, source_target_pairs={{0,1},{1,0},{2,3},{3,2},{4,5},{5,4},{6,7},{7,6},{8,9},{9,8},{10,11... | collective-permute-start | bytes 221192 | tf_op jit(solution)/shard_map/ppermute | solution.py:35
  13.3 5.4 %collective-permute-start.10 = (f16[304,128]{1,0:T(8,128)(2,1)S(1)}, f16[304,128]{1,0:T(8,128)(2,1)S(1)}, u32[]{:S(2)}, u32[]{:S(2)}) collective-permute-start(f16[304,128]{1,0:T(8,128)(2,1)S(1)} %multiply_convert_fusion), channel_id=1, source_target_pairs={{0,18},{1,13},{2,16},{3,15},{4,22},{5,9},{6,20},{7,11},{8,26},{9,5... | collective-permute-start | bytes 233480 | tf_op jit(solution)/shard_map/ppermute | solution.py:35
  15.8 4.4 %collective-permute-start.9 = (f16[304,128]{1,0:T(8,128)(2,1)S(1)}, f16[304,128]{1,0:T(8,128)(2,1)S(1)}, u32[]{:S(2)}, u32[]{:S(2)}) collective-permute-start(f16[304,128]{1,0:T(8,128)(2,1)S(1)} %multiply_convert_fusion.1), channel_id=1, source_target_pairs={{0,2},{1,5},{2,0},{3,7},{4,6},{5,1},{6,4},{7,3},{8,10},{9,13},{10,... | collective-permute-start | bytes 233480 | tf_op jit(solution)/shard_map/ppermute | solution.py:35
  16.3 4.4 %collective-permute-start.8 = (f16[304,128]{1,0:T(8,128)(2,1)S(1)}, f16[304,128]{1,0:T(8,128)(2,1)S(1)}, u32[]{:S(2)}, u32[]{:S(2)}) collective-permute-start(f16[304,128]{1,0:T(8,128)(2,1)S(1)} %multiply_convert_fusion.2), channel_id=1, source_target_pairs={{0,16},{1,9},{2,18},{3,11},{4,20},{5,13},{6,22},{7,15},{8,24},{9,1... | collective-permute-start | bytes 233480 | tf_op jit(solution)/shard_map/ppermute | solution.py:35
  20.8 1.3 %collective-permute-start.11 = (f32[152,128]{1,0:T(8,128)S(1)}, f32[152,128]{1,0:T(8,128)S(1)}, u32[]{:S(2)}, u32[]{:S(2)}) collective-permute-start(f32[152,128]{1,0:T(8,128)S(1)} %get-tuple-element.17), channel_id=1, source_target_pairs={{0,1},{1,0},{2,3},{3,2},{4,5},{5,4},{6,7},{7,6},{8,9},{9,8},{10,11... | collective-permute-start | bytes 233480 | tf_op jit(solution)/shard_map/ppermute | solution.py:35

commit v6 on v5

--- a/solution.py
+++ b/solution.py
@@ -81,7 +81,7 @@
     norm_out[...] = jnp.broadcast_to(norm, norm_out.shape)
 
 
-def tile_kernel(rows, scale_ref, shift_ref, mine, other, *outs):
+def tile_kernel(rows, lift, scale_ref, shift_ref, mine, other, *outs):
     scale = scale_ref[0]
     shift = shift_ref[0]
     own = mine[...]
@@ -104,13 +104,13 @@
     for slot, out in enumerate(outs):
         top = slot * size
         part = loss[:, top // LANES * LANES : top // LANES * LANES + LANES]
-        part = jnp.broadcast_to(part, (8, LANES))
+        part = jnp.broadcast_to(part, (8, LANES)) * (lift if slot else 1.0)
         if top % LANES:
             part = pltpu.roll(part, LANES - top % LANES, 1)
         for side in range(2):
             for chunk in range(chunks):
                 at = side * half + chunk * rows
-                out[at : at + rows, :] = grad[
+                out[at : at + rows, :] = (lift if slot else 1.0) * grad[
                     top + side * rows : top + (side + 1) * rows, chunk * LANES : (chunk + 1) * LANES
                 ]
             out[(side + 1) * half - 8 : (side + 1) * half, :] = part
@@ -184,22 +184,23 @@
     mine = jnp.concatenate([chip] + gathered, 0)
     other = jnp.concatenate([chip_other] + [permuted(part, devices, 1, 1) for part in gathered], 0)
     half = chunks * rows + 8
+    lift = message_lift(2 * rows * slots)
     message = jax.ShapeDtypeStruct((2 * half, LANES), jnp.float32)
     parts = pl.pallas_call(
-        functools.partial(tile_kernel, rows),
+        functools.partial(tile_kernel, rows, lift),
         out_shape=[message] * slots,
         in_specs=[pl.BlockSpec(memory_space=pltpu.SMEM)] * 2 + vmem(2),
         out_specs=vmem(slots),
         compiler_params=params,
         name="tile",
     )(scale.reshape(1), shift.reshape(1), mine, other)
-    lift = message_lift(2 * rows * slots)
-    whole = parts[0]
-    for part, (a, b) in zip(parts[1:], steps):
-        sent = (part * lift).astype(jnp.float16)
-        whole = whole + permuted(sent, devices, a, b).astype(jnp.float32) * (1.0 / lift)
-    kept = whole[:half]
-    came = permuted(whole[half:], devices, 1, 1)
+    arrived = [permuted(part.astype(jnp.float16), devices, a, b) for part, (a, b) in zip(parts[1:], steps)]
+
+    def total(span):
+        return sum((part[span].astype(jnp.float32) * (1.0 / lift) for part in arrived), parts[0][span])
+
+    came = permuted(total(slice(half, 2 * half)), devices, 1, 1)
+    kept = total(slice(0, half))
     return pl.pallas_call(
         functools.partial(finish_kernel, devices * rows),
         out_shape=(

time: 23.1 us -> 23.1 us (level)
  no operation moved by 1% of the time
where the time goes in v6:
time: 23.1 us; the launch traced here: 22.9 us
  starting transfers between devices  10.4 us (45%)
  waiting for transfers between devices  7.84 us (34%)
  between operations  2.01 us (9%)
  Pallas kernels  1.68 us (7%)
  local copies, waits for them, and re-layouts  0.78 us (3%)
    ppermute x12, starting transfers between devices, permuted(): return lax.ppermute(value, AXES, pairs)  10.4 us
    ppermute x12, waiting for transfers between devices, permuted(): return lax.ppermute(value, AXES, pairs)  7.84 us
    pallas_call x1, Pallas kernels, local(): pl.pallas_call(functools.partial(finish_kernel, devices * rows), out_shap...  0.78 us
    unnamed x3, local copies, waits for them, and re-layouts  0.77 us
    pallas_call x1, Pallas kernels, local(): pl.pallas_call(functools.partial(tile_kernel, rows, lift), out_shape=[mes...  0.54 us
  transfers between devices with their start and end apart: 12, of which 11 were waited for; matrix products, arithmetic and copies ran while one was open for 4% of the time, Pallas kernels for 1%

profile of v6, /device:TPU:0, one launch (start us, length us, event | category | flops | bytes accessed | tf_op | source)
XLA Modules:
  0.0 22.9 jit_solution(763621470197397679)
XLA Ops:
  0.6 0.0 copy-start
  0.6 0.5 %collective-permute-start = (bf16[16,1152]{1,0:T(8,128)(2,1)}, bf16[16,1152]{1,0:T(8,128)(2,1)S(1)}, u32[]{:S(2)}, u32[]{:S(2)}) collective-permute-start(bf16[16,1152]{1,0:T(8,128)(2,1)} %param.4), channel_id=1, source_target_pairs={{0,1},{1,0},{2,3},{3,2},{4,5},{5,4},{6,7},{7,6},{8,9},{9,8},{10,11... | collective-permute-start | bytes 110600 | tf_op jit(solution)/shard_map/ppermute | solution.py:35
  1.2 0.1 collective-permute-start.1
  1.2 0.8 %constant_dynamic-update-slice_fusion.1 = bf16[32,1152]{1,0:T(8,128)(2,1)S(1)} fusion(bf16[16,1152]{1,0:T(8,128)(2,1)} %param.4), kind=kLoop, calls=%fused_computation.5 | loop fusion | bytes 73728
  2.0 0.0 copy-done
  2.0 0.2 collective-permute-done.images_near
  2.2 0.3 %collective-permute-done.1.texts_near = bf16[16,1152]{1,0:T(8,128)(2,1)S(1)} collective-permute-done((bf16[16,1152]{1,0:T(8,128)(2,1)}, bf16[16,1152]{1,0:T(8,128)(2,1)S(1)}, u32[]{:S(2)}, u32[]{:S(2)}) %collective-permute-start.1) | collective-permute-done | bytes 36896 | tf_op jit(solution)/shard_map/ppermute | solution.py:35
  2.6 0.1 embed.1
  2.7 3.7 %collective-permute-start.4 = (bf16[32,1152]{1,0:T(8,128)(2,1)S(1)}, bf16[32,1152]{1,0:T(8,128)(2,1)S(1)}, u32[]{:S(2)}, u32[]{:S(2)}) collective-permute-start(bf16[32,1152]{1,0:T(8,128)(2,1)S(1)} %embed.1), channel_id=1, source_target_pairs={{0,18},{1,13},{2,16},{3,15},{4,22},{5,9},{6,20},{7,11},{8,26},{9,5... | collective-permute-start | bytes 221192 | tf_op jit(solution)/shard_map/ppermute | solution.py:35
  6.4 0.5 %collective-permute-start.3 = (bf16[32,1152]{1,0:T(8,128)(2,1)S(1)}, bf16[32,1152]{1,0:T(8,128)(2,1)S(1)}, u32[]{:S(2)}, u32[]{:S(2)}) collective-permute-start(bf16[32,1152]{1,0:T(8,128)(2,1)S(1)} %embed.1), channel_id=1, source_target_pairs={{0,2},{1,5},{2,0},{3,7},{4,6},{5,1},{6,4},{7,3},{8,10},{9,13},{10,... | collective-permute-start | bytes 221192 | tf_op jit(solution)/shard_map/ppermute | solution.py:35
  6.9 0.1 collective-permute-start.2
  8.3 0.2 %embed_other.1 = (bf16[32,1152]{1,0:T(8,128)(2,1)S(1)}, f32[32,1152]{1,0:T(8,128)S(1)}, f32[32,128]{1,0:T(8,128)S(1)}) custom-call(bf16[32,1152]{1,0:T(8,128)(2,1)S(1)} %constant_dynamic-update-slice_fusion.own, bf16[16,1152]{1,0:T(8,128)(2,1)S(1)} %collective-permute-done.images_near, bf16[16,1152]{1,0:T(8,128)(2,1)S(1)} %collective-permute-done.1.texts_near), custom_call_target="tpu_custom_call" | custom-call | tf_op jit(solution)/shard_map/embed_other/pallas_call | solution.py:170
  8.6 0.1 collective-permute-done.4
  8.7 0.9 %collective-permute-start.7 = (bf16[32,1152]{1,0:T(8,128)(2,1)S(1)}, bf16[32,1152]{1,0:T(8,128)(2,1)S(1)}, u32[]{:S(2)}, u32[]{:S(2)}) collective-permute-start(bf16[32,1152]{1,0:T(8,128)(2,1)S(1)} %collective-permute-done.4), channel_id=1, source_target_pairs={{0,1},{1,0},{2,3},{3,2},{4,5},{5,4},{6,7},{7,6},{8,9},{9,8},{10,11... | collective-permute-start | bytes 221192 | tf_op jit(solution)/shard_map/ppermute | solution.py:35
  9.6 1.1 %collective-permute-done.3 = bf16[32,1152]{1,0:T(8,128)(2,1)S(1)} collective-permute-done((bf16[32,1152]{1,0:T(8,128)(2,1)S(1)}, bf16[32,1152]{1,0:T(8,128)(2,1)S(1)}, u32[]{:S(2)}, u32[]{:S(2)}) %collective-permute-start.3) | collective-permute-done | bytes 73760 | tf_op jit(solution)/shard_map/ppermute | solution.py:35
  10.7 0.4 %collective-permute-start.6 = (bf16[32,1152]{1,0:T(8,128)(2,1)S(1)}, bf16[32,1152]{1,0:T(8,128)(2,1)S(1)}, u32[]{:S(2)}, u32[]{:S(2)}) collective-permute-start(bf16[32,1152]{1,0:T(8,128)(2,1)S(1)} %collective-permute-done.3), channel_id=1, source_target_pairs={{0,1},{1,0},{2,3},{3,2},{4,5},{5,4},{6,7},{7,6},{8,9},{9,8},{10,11... | collective-permute-start | bytes 221192 | tf_op jit(solution)/shard_map/ppermute | solution.py:35
  11.1 0.1 collective-permute-done.2
  11.2 0.5 %collective-permute-start.5 = (bf16[32,1152]{1,0:T(8,128)(2,1)S(1)}, bf16[32,1152]{1,0:T(8,128)(2,1)S(1)}, u32[]{:S(2)}, u32[]{:S(2)}) collective-permute-start(bf16[32,1152]{1,0:T(8,128)(2,1)S(1)} %collective-permute-done.2), channel_id=1, source_target_pairs={{0,1},{1,0},{2,3},{3,2},{4,5},{5,4},{6,7},{7,6},{8,9},{9,8},{10,11... | collective-permute-start | bytes 221192 | tf_op jit(solution)/shard_map/ppermute | solution.py:35
  11.7 0.0 collective-permute-done.7
  11.7 0.3 %collective-permute-done.6 = bf16[32,1152]{1,0:T(8,128)(2,1)S(1)} collective-permute-done((bf16[32,1152]{1,0:T(8,128)(2,1)S(1)}, bf16[32,1152]{1,0:T(8,128)(2,1)S(1)}, u32[]{:S(2)}, u32[]{:S(2)}) %collective-permute-start.6) | collective-permute-done | bytes 73760 | tf_op jit(solution)/shard_map/ppermute | solution.py:35
  12.0 0.6 %collective-permute-done.5 = bf16[32,1152]{1,0:T(8,128)(2,1)S(1)} collective-permute-done((bf16[32,1152]{1,0:T(8,128)(2,1)S(1)}, bf16[32,1152]{1,0:T(8,128)(2,1)S(1)}, u32[]{:S(2)}, u32[]{:S(2)}) %collective-permute-start.5) | collective-permute-done | bytes 73760 | tf_op jit(solution)/shard_map/ppermute | solution.py:35
  12.6 0.5 %tile.1 = (f32[304,128]{1,0:T(8,128)S(1)}, f32[304,128]{1,0:T(8,128)S(1)}, f32[304,128]{1,0:T(8,128)S(1)}, f32[304,128]{1,0:T(8,128)S(1)}) custom-call(f32[1]{0:T(128)} %bitcast.2.scale_ref, f32[1]{0:T(128)} %bitcast.3.shift_ref, bf16[128,1152]{1,0:T(8,128)(2,1)S(1)} %pad_maximum_fusion.mine, bf16[128,1152]{1,0:T(8,128)(2,1)S(1)} %pad_maximum_fusion.1.other), custom_call_target="tpu_custom_call" | custom-call | tf_op jit(solution)/shard_map/tile/pallas_call | solution.py:189
  13.3 2.5 %collective-permute-start.10 = (f16[304,128]{1,0:T(8,128)(2,1)S(1)}, f16[304,128]{1,0:T(8,128)(2,1)S(1)}, u32[]{:S(2)}, u32[]{:S(2)}) collective-permute-start(f16[304,128]{1,0:T(8,128)(2,1)S(1)} %convert_element_type.31), channel_id=1, source_target_pairs={{0,18},{1,13},{2,16},{3,15},{4,22},{5,9},{6,20},{7,11},{8,26},{9,5... | collective-permute-start | bytes 233480 | tf_op jit(solution)/shard_map/ppermute | solution.py:35
  15.8 0.5 %collective-permute-start.9 = (f16[304,128]{1,0:T(8,128)(2,1)S(1)}, f16[304,128]{1,0:T(8,128)(2,1)S(1)}, u32[]{:S(2)}, u32[]{:S(2)}) collective-permute-start(f16[304,128]{1,0:T(8,128)(2,1)S(1)} %convert_element_type.29), channel_id=1, source_target_pairs={{0,2},{1,5},{2,0},{3,7},{4,6},{5,1},{6,4},{7,3},{8,10},{9,13},{10,... | collective-permute-start | bytes 233480 | tf_op jit(solution)/shard_map/ppermute | solution.py:35
  16.3 0.5 %collective-permute-start.8 = (f16[304,128]{1,0:T(8,128)(2,1)S(1)}, f16[304,128]{1,0:T(8,128)(2,1)S(1)}, u32[]{:S(2)}, u32[]{:S(2)}) collective-permute-start(f16[304,128]{1,0:T(8,128)(2,1)S(1)} %convert_element_type.27), channel_id=1, source_target_pairs={{0,16},{1,9},{2,18},{3,11},{4,20},{5,13},{6,22},{7,15},{8,24},{9,1... | collective-permute-start | bytes 233480 | tf_op jit(solution)/shard_map/ppermute | solution.py:35
  16.8 1.8 %collective-permute-done.10 = f16[304,128]{1,0:T(8,128)(2,1)S(1)} collective-permute-done((f16[304,128]{1,0:T(8,128)(2,1)S(1)}, f16[304,128]{1,0:T(8,128)(2,1)S(1)}, u32[]{:S(2)}, u32[]{:S(2)}) %collective-permute-start.10) | collective-permute-done | bytes 77856 | tf_op jit(solution)/shard_map/ppermute | solution.py:35
  18.6 1.5 %collective-permute-done.9 = f16[304,128]{1,0:T(8,128)(2,1)S(1)} collective-permute-done((f16[304,128]{1,0:T(8,128)(2,1)S(1)}, f16[304,128]{1,0:T(8,128)(2,1)S(1)}, u32[]{:S(2)}, u32[]{:S(2)}) %collective-permute-start.9) | collective-permute-done | bytes 77856 | tf_op jit(solution)/shard_map/ppermute | solution.py:35
  20.2 0.5 %collective-permute-done.8 = f16[304,128]{1,0:T(8,128)(2,1)S(1)} collective-permute-done((f16[304,128]{1,0:T(8,128)(2,1)S(1)}, f16[304,128]{1,0:T(8,128)(2,1)S(1)}, u32[]{:S(2)}, u32[]{:S(2)}) %collective-permute-start.8) | collective-permute-done | bytes 77856 | tf_op jit(solution)/shard_map/ppermute | solution.py:35
  20.7 0.1 multiply_add_fusion
  20.7 0.2 %collective-permute-start.11 = (f32[152,128]{1,0:T(8,128)S(1)}, f32[152,128]{1,0:T(8,128)S(1)}, u32[]{:S(2)}, u32[]{:S(2)}) collective-permute-start(f32[152,128]{1,0:T(8,128)S(1)} %get-tuple-element.17), channel_id=1, source_target_pairs={{0,1},{1,0},{2,3},{3,2},{4,5},{5,4},{6,7},{7,6},{8,9},{9,8},{10,11... | collective-permute-start | bytes 233480 | tf_op jit(solution)/shard_map/ppermute | solution.py:35
  21.0 1.1 %collective-permute-done.11.came = f32[152,128]{1,0:T(8,128)S(1)} collective-permute-done((f32[152,128]{1,0:T(8,128)S(1)}, f32[152,128]{1,0:T(8,128)S(1)}, u32[]{:S(2)}, u32[]{:S(2)}) %collective-permute-start.11) | collective-permute-done | bytes 77856 | tf_op jit(solution)/shard_map/ppermute | solution.py:35
  22.1 0.8 %finish.1 = (f32[16]{0:T(128)}, f32[16,1152]{1,0:T(8,128)}, f32[16,1152]{1,0:T(8,128)}) custom-call(f32[32,1152]{1,0:T(8,128)S(1)} %get-tuple-element.10.unit, f32[32,128]{1,0:T(8,128)S(1)} %get-tuple-element.11.norm, f32[152,128]{1,0:T(8,128)S(1)} %get-tuple-element.18.kept, f32[152,128]{1,0:T(8,128)S(1)} %collective-permute-done.11.came), custom_call_target="tpu_custom_call" | custom-call | tf_op jit(solution)/shard_map/finish/pallas_call | solution.py:204
  (6 shorter events, 0.1 us)
Async XLA Ops:
  0.6 1.4 %copy-start = (bf16[16,1152]{1,0:T(8,128)(2,1)S(1)}, bf16[16,1152]{1,0:T(8,128)(2,1)}, u32[]{:S(2)}) copy-start(bf16[16,1152]{1,0:T(8,128)(2,1)} %param.5) | copy-start | bytes 110596
  0.6 1.6 %collective-permute-start = (bf16[16,1152]{1,0:T(8,128)(2,1)}, bf16[16,1152]{1,0:T(8,128)(2,1)S(1)}, u32[]{:S(2)}, u32[]{:S(2)}) collective-permute-start(bf16[16,1152]{1,0:T(8,128)(2,1)} %param.4), channel_id=1, source_target_pairs={{0,1},{1,0},{2,3},{3,2},{4,5},{5,4},{6,7},{7,6},{8,9},{9,8},{10,11... | collective-permute-start | bytes 110600 | tf_op jit(solution)/shard_map/ppermute | solution.py:35
  1.2 1.4 %collective-permute-start.1 = (bf16[16,1152]{1,0:T(8,128)(2,1)}, bf16[16,1152]{1,0:T(8,128)(2,1)S(1)}, u32[]{:S(2)}, u32[]{:S(2)}) collective-permute-start(bf16[16,1152]{1,0:T(8,128)(2,1)} %param.5), channel_id=1, source_target_pairs={{0,1},{1,0},{2,3},{3,2},{4,5},{5,4},{6,7},{7,6},{8,9},{9,8},{10,11... | collective-permute-start | bytes 110600 | tf_op jit(solution)/shard_map/ppermute | solution.py:35
  2.7 6.0 %collective-permute-start.4 = (bf16[32,1152]{1,0:T(8,128)(2,1)S(1)}, bf16[32,1152]{1,0:T(8,128)(2,1)S(1)}, u32[]{:S(2)}, u32[]{:S(2)}) collective-permute-start(bf16[32,1152]{1,0:T(8,128)(2,1)S(1)} %embed.1), channel_id=1, source_target_pairs={{0,18},{1,13},{2,16},{3,15},{4,22},{5,9},{6,20},{7,11},{8,26},{9,5... | collective-permute-start | bytes 221192 | tf_op jit(solution)/shard_map/ppermute | solution.py:35
  6.4 4.4 %collective-permute-start.3 = (bf16[32,1152]{1,0:T(8,128)(2,1)S(1)}, bf16[32,1152]{1,0:T(8,128)(2,1)S(1)}, u32[]{:S(2)}, u32[]{:S(2)}) collective-permute-start(bf16[32,1152]{1,0:T(8,128)(2,1)S(1)} %embed.1), channel_id=1, source_target_pairs={{0,2},{1,5},{2,0},{3,7},{4,6},{5,1},{6,4},{7,3},{8,10},{9,13},{10,... | collective-permute-start | bytes 221192 | tf_op jit(solution)/shard_map/ppermute | solution.py:35
  6.9 4.4 %collective-permute-start.2 = (bf16[32,1152]{1,0:T(8,128)(2,1)S(1)}, bf16[32,1152]{1,0:T(8,128)(2,1)S(1)}, u32[]{:S(2)}, u32[]{:S(2)}) collective-permute-start(bf16[32,1152]{1,0:T(8,128)(2,1)S(1)} %embed.1), channel_id=1, source_target_pairs={{0,16},{1,9},{2,18},{3,11},{4,20},{5,13},{6,22},{7,15},{8,24},{9,1... | collective-permute-start | bytes 221192 | tf_op jit(solution)/shard_map/ppermute | solution.py:35
  8.7 3.0 %collective-permute-start.7 = (bf16[32,1152]{1,0:T(8,128)(2,1)S(1)}, bf16[32,1152]{1,0:T(8,128)(2,1)S(1)}, u32[]{:S(2)}, u32[]{:S(2)}) collective-permute-start(bf16[32,1152]{1,0:T(8,128)(2,1)S(1)} %collective-permute-done.4), channel_id=1, source_target_pairs={{0,1},{1,0},{2,3},{3,2},{4,5},{5,4},{6,7},{7,6},{8,9},{9,8},{10,11... | collective-permute-start | bytes 221192 | tf_op jit(solution)/shard_map/ppermute | solution.py:35
  10.7 1.3 %collective-permute-start.6 = (bf16[32,1152]{1,0:T(8,128)(2,1)S(1)}, bf16[32,1152]{1,0:T(8,128)(2,1)S(1)}, u32[]{:S(2)}, u32[]{:S(2)}) collective-permute-start(bf16[32,1152]{1,0:T(8,128)(2,1)S(1)} %collective-permute-done.3), channel_id=1, source_target_pairs={{0,1},{1,0},{2,3},{3,2},{4,5},{5,4},{6,7},{7,6},{8,9},{9,8},{10,11... | collective-permute-start | bytes 221192 | tf_op jit(solution)/shard_map/ppermute | solution.py:35
  11.2 1.4 %collective-permute-start.5 = (bf16[32,1152]{1,0:T(8,128)(2,1)S(1)}, bf16[32,1152]{1,0:T(8,128)(2,1)S(1)}, u32[]{:S(2)}, u32[]{:S(2)}) collective-permute-start(bf16[32,1152]{1,0:T(8,128)(2,1)S(1)} %collective-permute-done.2), channel_id=1, source_target_pairs={{0,1},{1,0},{2,3},{3,2},{4,5},{5,4},{6,7},{7,6},{8,9},{9,8},{10,11... | collective-permute-start | bytes 221192 | tf_op jit(solution)/shard_map/ppermute | solution.py:35
  13.3 5.4 %collective-permute-start.10 = (f16[304,128]{1,0:T(8,128)(2,1)S(1)}, f16[304,128]{1,0:T(8,128)(2,1)S(1)}, u32[]{:S(2)}, u32[]{:S(2)}) collective-permute-start(f16[304,128]{1,0:T(8,128)(2,1)S(1)} %convert_element_type.31), channel_id=1, source_target_pairs={{0,18},{1,13},{2,16},{3,15},{4,22},{5,9},{6,20},{7,11},{8,26},{9,5... | collective-permute-start | bytes 233480 | tf_op jit(solution)/shard_map/ppermute | solution.py:35
  15.8 4.4 %collective-permute-start.9 = (f16[304,128]{1,0:T(8,128)(2,1)S(1)}, f16[304,128]{1,0:T(8,128)(2,1)S(1)}, u32[]{:S(2)}, u32[]{:S(2)}) collective-permute-start(f16[304,128]{1,0:T(8,128)(2,1)S(1)} %convert_element_type.29), channel_id=1, source_target_pairs={{0,2},{1,5},{2,0},{3,7},{4,6},{5,1},{6,4},{7,3},{8,10},{9,13},{10,... | collective-permute-start | bytes 233480 | tf_op jit(solution)/shard_map/ppermute | solution.py:35
  16.3 4.4 %collective-permute-start.8 = (f16[304,128]{1,0:T(8,128)(2,1)S(1)}, f16[304,128]{1,0:T(8,128)(2,1)S(1)}, u32[]{:S(2)}, u32[]{:S(2)}) collective-permute-start(f16[304,128]{1,0:T(8,128)(2,1)S(1)} %convert_element_type.27), channel_id=1, source_target_pairs={{0,16},{1,9},{2,18},{3,11},{4,20},{5,13},{6,22},{7,15},{8,24},{9,1... | collective-permute-start | bytes 233480 | tf_op jit(solution)/shard_map/ppermute | solution.py:35
  20.7 1.3 %collective-permute-start.11 = (f32[152,128]{1,0:T(8,128)S(1)}, f32[152,128]{1,0:T(8,128)S(1)}, u32[]{:S(2)}, u32[]{:S(2)}) collective-permute-start(f32[152,128]{1,0:T(8,128)S(1)} %get-tuple-element.17), channel_id=1, source_target_pairs={{0,1},{1,0},{2,3},{3,2},{4,5},{5,4},{6,7},{7,6},{8,9},{9,8},{10,11... | collective-permute-start | bytes 233480 | tf_op jit(solution)/shard_map/ppermute | solution.py:35

commit v7 on v6

--- a/solution.py
+++ b/solution.py
@@ -30,8 +30,8 @@
     return [(spread(k, image_bits), spread(k, text_bits)) for k in [*range(last - 1, 0, -1), last]]
 
 
-def permuted(value, devices, image_step, text_step):
-    pairs = [(d, d ^ (text_step if d & 1 else image_step)) for d in range(devices)]
+def permuted(value, devices, image_step, text_step, cross=0):
+    pairs = [(d, d ^ (text_step if d & 1 else image_step) ^ cross) for d in range(devices)]
     return lax.ppermute(value, AXES, pairs)
 
 
@@ -84,8 +84,9 @@
 def tile_kernel(rows, lift, scale_ref, shift_ref, mine, other, *outs):
     scale = scale_ref[0]
     shift = shift_ref[0]
-    own = mine[...]
-    far = other[...]
+    top = mine.shape[0] - 2 * rows
+    own = jnp.concatenate([mine[:top, :], other[top:, :]], 0)
+    far = jnp.concatenate([other[:top, :], mine[top:, :]], 0)
     count = own.shape[0]
     size = 2 * rows
     nt = (((1,), (1,)), ((), ()))
@@ -179,7 +180,7 @@
         compiler_params=params,
         name="embed_other",
     )(*raws)
-    gathered = [permuted(chip, devices, a, b) for a, b in steps]
+    gathered = [permuted(chip, devices, a, b, int((a, b) == steps[-1])) for a, b in steps]
     slots = len(steps) + 1
     mine = jnp.concatenate([chip] + gathered, 0)
     other = jnp.concatenate([chip_other] + [permuted(part, devices, 1, 1) for part in gathered], 0)

time: 23.1 us -> 23.1 us (level)
  waiting for transfers between devices: 7.84 us -> 8.59 us
  starting transfers between devices: 10.4 us -> 9.67 us
    ppermute x12, waiting for transfers between devices: 7.84 us -> 8.59 us  [permuted(): return lax.ppermute(value, AXES, pairs)]
    ppermute x12, starting transfers between devices: 10.4 us -> 9.67 us  [permuted(): return lax.ppermute(value, AXES, pairs)]
  transfers between devices with their start and end apart: 12 -> 12, of which waited for: 11 -> 10; matrix products, arithmetic and copies ran while one was open for 4% -> 4% of each run, Pallas kernels for 1% -> 1%
where the time goes in v7:
time: 23.1 us; the launch traced here: 22.9 us
  starting transfers between devices  9.67 us (42%)
  waiting for transfers between devices  8.59 us (37%)
  between operations  2.01 us (9%)
  Pallas kernels  1.68 us (7%)
  local copies, waits for them, and re-layouts  0.78 us (3%)
    ppermute x12, starting transfers between devices, permuted(): return lax.ppermute(value, AXES, pairs)  9.67 us
    ppermute x12, waiting for transfers between devices, permuted(): return lax.ppermute(value, AXES, pairs)  8.59 us
    pallas_call x1, Pallas kernels, local(): pl.pallas_call(functools.partial(finish_kernel, devices * rows), out_shap...  0.78 us
    unnamed x3, local copies, waits for them, and re-layouts  0.77 us
    pallas_call x1, Pallas kernels, local(): pl.pallas_call(functools.partial(tile_kernel, rows, lift), out_shape=[mes...  0.54 us
  transfers between devices with their start and end apart: 12, of which 10 were waited for; matrix products, arithmetic and copies ran while one was open for 4% of the time, Pallas kernels for 1%

profile of v7, /device:TPU:0, one launch (start us, length us, event | category | flops | bytes accessed | tf_op | source)
XLA Modules:
  0.0 22.9 jit_solution(1144885373379561286)
XLA Ops:
  0.6 0.0 copy-start
  0.6 0.5 %collective-permute-start = (bf16[16,1152]{1,0:T(8,128)(2,1)}, bf16[16,1152]{1,0:T(8,128)(2,1)S(1)}, u32[]{:S(2)}, u32[]{:S(2)}) collective-permute-start(bf16[16,1152]{1,0:T(8,128)(2,1)} %param.4), channel_id=1, source_target_pairs={{0,1},{1,0},{2,3},{3,2},{4,5},{5,4},{6,7},{7,6},{8,9},{9,8},{10,11... | collective-permute-start | bytes 110600 | tf_op jit(solution)/shard_map/ppermute | solution.py:35
  1.2 0.1 collective-permute-start.1
  1.2 0.8 %constant_dynamic-update-slice_fusion.1 = bf16[32,1152]{1,0:T(8,128)(2,1)S(1)} fusion(bf16[16,1152]{1,0:T(8,128)(2,1)} %param.4), kind=kLoop, calls=%fused_computation.5 | loop fusion | bytes 73728
  2.0 0.0 copy-done
  2.0 0.2 collective-permute-done.images_near
  2.2 0.3 %collective-permute-done.1.texts_near = bf16[16,1152]{1,0:T(8,128)(2,1)S(1)} collective-permute-done((bf16[16,1152]{1,0:T(8,128)(2,1)}, bf16[16,1152]{1,0:T(8,128)(2,1)S(1)}, u32[]{:S(2)}, u32[]{:S(2)}) %collective-permute-start.1) | collective-permute-done | bytes 36896 | tf_op jit(solution)/shard_map/ppermute | solution.py:35
  2.6 0.1 embed.1
  2.7 3.6 %collective-permute-start.4 = (bf16[32,1152]{1,0:T(8,128)(2,1)S(1)}, bf16[32,1152]{1,0:T(8,128)(2,1)S(1)}, u32[]{:S(2)}, u32[]{:S(2)}) collective-permute-start(bf16[32,1152]{1,0:T(8,128)(2,1)S(1)} %embed.1), channel_id=1, source_target_pairs={{0,19},{1,12},{2,17},{3,14},{4,23},{5,8},{6,21},{7,10},{8,27},{9,4... | collective-permute-start | bytes 221192 | tf_op jit(solution)/shard_map/ppermute | solution.py:35
  6.3 0.5 %collective-permute-start.3 = (bf16[32,1152]{1,0:T(8,128)(2,1)S(1)}, bf16[32,1152]{1,0:T(8,128)(2,1)S(1)}, u32[]{:S(2)}, u32[]{:S(2)}) collective-permute-start(bf16[32,1152]{1,0:T(8,128)(2,1)S(1)} %embed.1), channel_id=1, source_target_pairs={{0,2},{1,5},{2,0},{3,7},{4,6},{5,1},{6,4},{7,3},{8,10},{9,13},{10,... | collective-permute-start | bytes 221192 | tf_op jit(solution)/shard_map/ppermute | solution.py:35
  6.8 0.2 collective-permute-start.2
  8.3 0.2 %embed_other.1 = (bf16[32,1152]{1,0:T(8,128)(2,1)S(1)}, f32[32,1152]{1,0:T(8,128)S(1)}, f32[32,128]{1,0:T(8,128)S(1)}) custom-call(bf16[32,1152]{1,0:T(8,128)(2,1)S(1)} %constant_dynamic-update-slice_fusion.own, bf16[16,1152]{1,0:T(8,128)(2,1)S(1)} %collective-permute-done.images_near, bf16[16,1152]{1,0:T(8,128)(2,1)S(1)} %collective-permute-done.1.texts_near), custom_call_target="tpu_custom_call" | custom-call | tf_op jit(solution)/shard_map/embed_other/pallas_call | solution.py:171
  8.6 0.9 %collective-permute-done.4 = bf16[32,1152]{1,0:T(8,128)(2,1)S(1)} collective-permute-done((bf16[32,1152]{1,0:T(8,128)(2,1)S(1)}, bf16[32,1152]{1,0:T(8,128)(2,1)S(1)}, u32[]{:S(2)}, u32[]{:S(2)}) %collective-permute-start.4) | collective-permute-done | bytes 73760 | tf_op jit(solution)/shard_map/ppermute | solution.py:35
  9.5 0.1 collective-permute-start.7
  9.6 1.1 %collective-permute-done.3 = bf16[32,1152]{1,0:T(8,128)(2,1)S(1)} collective-permute-done((bf16[32,1152]{1,0:T(8,128)(2,1)S(1)}, bf16[32,1152]{1,0:T(8,128)(2,1)S(1)}, u32[]{:S(2)}, u32[]{:S(2)}) %collective-permute-start.3) | collective-permute-done | bytes 73760 | tf_op jit(solution)/shard_map/ppermute | solution.py:35
  10.7 0.5 %collective-permute-start.6 = (bf16[32,1152]{1,0:T(8,128)(2,1)S(1)}, bf16[32,1152]{1,0:T(8,128)(2,1)S(1)}, u32[]{:S(2)}, u32[]{:S(2)}) collective-permute-start(bf16[32,1152]{1,0:T(8,128)(2,1)S(1)} %collective-permute-done.3), channel_id=1, source_target_pairs={{0,1},{1,0},{2,3},{3,2},{4,5},{5,4},{6,7},{7,6},{8,9},{9,8},{10,11... | collective-permute-start | bytes 221192 | tf_op jit(solution)/shard_map/ppermute | solution.py:35
  11.1 0.0 collective-permute-done.2
  11.2 0.6 %collective-permute-start.5 = (bf16[32,1152]{1,0:T(8,128)(2,1)S(1)}, bf16[32,1152]{1,0:T(8,128)(2,1)S(1)}, u32[]{:S(2)}, u32[]{:S(2)}) collective-permute-start(bf16[32,1152]{1,0:T(8,128)(2,1)S(1)} %collective-permute-done.2), channel_id=1, source_target_pairs={{0,1},{1,0},{2,3},{3,2},{4,5},{5,4},{6,7},{7,6},{8,9},{9,8},{10,11... | collective-permute-start | bytes 221192 | tf_op jit(solution)/shard_map/ppermute | solution.py:35
  11.8 0.0 collective-permute-done.7
  11.8 0.3 %collective-permute-done.6 = bf16[32,1152]{1,0:T(8,128)(2,1)S(1)} collective-permute-done((bf16[32,1152]{1,0:T(8,128)(2,1)S(1)}, bf16[32,1152]{1,0:T(8,128)(2,1)S(1)}, u32[]{:S(2)}, u32[]{:S(2)}) %collective-permute-start.6) | collective-permute-done | bytes 73760 | tf_op jit(solution)/shard_map/ppermute | solution.py:35
  12.0 0.6 %collective-permute-done.5 = bf16[32,1152]{1,0:T(8,128)(2,1)S(1)} collective-permute-done((bf16[32,1152]{1,0:T(8,128)(2,1)S(1)}, bf16[32,1152]{1,0:T(8,128)(2,1)S(1)}, u32[]{:S(2)}, u32[]{:S(2)}) %collective-permute-start.5) | collective-permute-done | bytes 73760 | tf_op jit(solution)/shard_map/ppermute | solution.py:35
  12.7 0.5 %tile.1 = (f32[304,128]{1,0:T(8,128)S(1)}, f32[304,128]{1,0:T(8,128)S(1)}, f32[304,128]{1,0:T(8,128)S(1)}, f32[304,128]{1,0:T(8,128)S(1)}) custom-call(f32[1]{0:T(128)} %bitcast.2.scale_ref, f32[1]{0:T(128)} %bitcast.3.shift_ref, bf16[128,1152]{1,0:T(8,128)(2,1)S(1)} %pad_maximum_fusion.mine, bf16[128,1152]{1,0:T(8,128)(2,1)S(1)} %pad_maximum_fusion.1.other), custom_call_target="tpu_custom_call" | custom-call | tf_op jit(solution)/shard_map/tile/pallas_call | solution.py:190
  13.3 2.5 %collective-permute-start.10 = (f16[304,128]{1,0:T(8,128)(2,1)S(1)}, f16[304,128]{1,0:T(8,128)(2,1)S(1)}, u32[]{:S(2)}, u32[]{:S(2)}) collective-permute-start(f16[304,128]{1,0:T(8,128)(2,1)S(1)} %convert_element_type.31), channel_id=1, source_target_pairs={{0,18},{1,13},{2,16},{3,15},{4,22},{5,9},{6,20},{7,11},{8,26},{9,5... | collective-permute-start | bytes 233480 | tf_op jit(solution)/shard_map/ppermute | solution.py:35
  15.8 0.5 %collective-permute-start.9 = (f16[304,128]{1,0:T(8,128)(2,1)S(1)}, f16[304,128]{1,0:T(8,128)(2,1)S(1)}, u32[]{:S(2)}, u32[]{:S(2)}) collective-permute-start(f16[304,128]{1,0:T(8,128)(2,1)S(1)} %convert_element_type.29), channel_id=1, source_target_pairs={{0,2},{1,5},{2,0},{3,7},{4,6},{5,1},{6,4},{7,3},{8,10},{9,13},{10,... | collective-permute-start | bytes 233480 | tf_op jit(solution)/shard_map/ppermute | solution.py:35
  16.3 0.5 %collective-permute-start.8 = (f16[304,128]{1,0:T(8,128)(2,1)S(1)}, f16[304,128]{1,0:T(8,128)(2,1)S(1)}, u32[]{:S(2)}, u32[]{:S(2)}) collective-permute-start(f16[304,128]{1,0:T(8,128)(2,1)S(1)} %convert_element_type.27), channel_id=1, source_target_pairs={{0,16},{1,9},{2,18},{3,11},{4,20},{5,13},{6,22},{7,15},{8,24},{9,1... | collective-permute-start | bytes 233480 | tf_op jit(solution)/shard_map/ppermute | solution.py:35
  16.8 1.8 %collective-permute-done.10 = f16[304,128]{1,0:T(8,128)(2,1)S(1)} collective-permute-done((f16[304,128]{1,0:T(8,128)(2,1)S(1)}, f16[304,128]{1,0:T(8,128)(2,1)S(1)}, u32[]{:S(2)}, u32[]{:S(2)}) %collective-permute-start.10) | collective-permute-done | bytes 77856 | tf_op jit(solution)/shard_map/ppermute | solution.py:35
  18.7 1.5 %collective-permute-done.9 = f16[304,128]{1,0:T(8,128)(2,1)S(1)} collective-permute-done((f16[304,128]{1,0:T(8,128)(2,1)S(1)}, f16[304,128]{1,0:T(8,128)(2,1)S(1)}, u32[]{:S(2)}, u32[]{:S(2)}) %collective-permute-start.9) | collective-permute-done | bytes 77856 | tf_op jit(solution)/shard_map/ppermute | solution.py:35
  20.2 0.5 %collective-permute-done.8 = f16[304,128]{1,0:T(8,128)(2,1)S(1)} collective-permute-done((f16[304,128]{1,0:T(8,128)(2,1)S(1)}, f16[304,128]{1,0:T(8,128)(2,1)S(1)}, u32[]{:S(2)}, u32[]{:S(2)}) %collective-permute-start.8) | collective-permute-done | bytes 77856 | tf_op jit(solution)/shard_map/ppermute | solution.py:35
  20.7 0.1 multiply_add_fusion
  20.8 0.1 collective-permute-start.11
  20.9 1.2 %collective-permute-done.11.came = f32[152,128]{1,0:T(8,128)S(1)} collective-permute-done((f32[152,128]{1,0:T(8,128)S(1)}, f32[152,128]{1,0:T(8,128)S(1)}, u32[]{:S(2)}, u32[]{:S(2)}) %collective-permute-start.11) | collective-permute-done | bytes 77856 | tf_op jit(solution)/shard_map/ppermute | solution.py:35
  22.1 0.8 %finish.1 = (f32[16]{0:T(128)}, f32[16,1152]{1,0:T(8,128)}, f32[16,1152]{1,0:T(8,128)}) custom-call(f32[32,1152]{1,0:T(8,128)S(1)} %get-tuple-element.10.unit, f32[32,128]{1,0:T(8,128)S(1)} %get-tuple-element.11.norm, f32[152,128]{1,0:T(8,128)S(1)} %get-tuple-element.18.kept, f32[152,128]{1,0:T(8,128)S(1)} %collective-permute-done.11.came), custom_call_target="tpu_custom_call" | custom-call | tf_op jit(solution)/shard_map/finish/pallas_call | solution.py:205
  (6 shorter events, 0.1 us)
Async XLA Ops:
  0.6 1.4 %copy-start = (bf16[16,1152]{1,0:T(8,128)(2,1)S(1)}, bf16[16,1152]{1,0:T(8,128)(2,1)}, u32[]{:S(2)}) copy-start(bf16[16,1152]{1,0:T(8,128)(2,1)} %param.5) | copy-start | bytes 110596
  0.6 1.6 %collective-permute-start = (bf16[16,1152]{1,0:T(8,128)(2,1)}, bf16[16,1152]{1,0:T(8,128)(2,1)S(1)}, u32[]{:S(2)}, u32[]{:S(2)}) collective-permute-start(bf16[16,1152]{1,0:T(8,128)(2,1)} %param.4), channel_id=1, source_target_pairs={{0,1},{1,0},{2,3},{3,2},{4,5},{5,4},{6,7},{7,6},{8,9},{9,8},{10,11... | collective-permute-start | bytes 110600 | tf_op jit(solution)/shard_map/ppermute | solution.py:35
  1.2 1.4 %collective-permute-start.1 = (bf16[16,1152]{1,0:T(8,128)(2,1)}, bf16[16,1152]{1,0:T(8,128)(2,1)S(1)}, u32[]{:S(2)}, u32[]{:S(2)}) collective-permute-start(bf16[16,1152]{1,0:T(8,128)(2,1)} %param.5), channel_id=1, source_target_pairs={{0,1},{1,0},{2,3},{3,2},{4,5},{5,4},{6,7},{7,6},{8,9},{9,8},{10,11... | collective-permute-start | bytes 110600 | tf_op jit(solution)/shard_map/ppermute | solution.py:35
  2.7 6.8 %collective-permute-start.4 = (bf16[32,1152]{1,0:T(8,128)(2,1)S(1)}, bf16[32,1152]{1,0:T(8,128)(2,1)S(1)}, u32[]{:S(2)}, u32[]{:S(2)}) collective-permute-start(bf16[32,1152]{1,0:T(8,128)(2,1)S(1)} %embed.1), channel_id=1, source_target_pairs={{0,19},{1,12},{2,17},{3,14},{4,23},{5,8},{6,21},{7,10},{8,27},{9,4... | collective-permute-start | bytes 221192 | tf_op jit(solution)/shard_map/ppermute | solution.py:35
  6.3 4.4 %collective-permute-start.3 = (bf16[32,1152]{1,0:T(8,128)(2,1)S(1)}, bf16[32,1152]{1,0:T(8,128)(2,1)S(1)}, u32[]{:S(2)}, u32[]{:S(2)}) collective-permute-start(bf16[32,1152]{1,0:T(8,128)(2,1)S(1)} %embed.1), channel_id=1, source_target_pairs={{0,2},{1,5},{2,0},{3,7},{4,6},{5,1},{6,4},{7,3},{8,10},{9,13},{10,... | collective-permute-start | bytes 221192 | tf_op jit(solution)/shard_map/ppermute | solution.py:35
  6.8 4.4 %collective-permute-start.2 = (bf16[32,1152]{1,0:T(8,128)(2,1)S(1)}, bf16[32,1152]{1,0:T(8,128)(2,1)S(1)}, u32[]{:S(2)}, u32[]{:S(2)}) collective-permute-start(bf16[32,1152]{1,0:T(8,128)(2,1)S(1)} %embed.1), channel_id=1, source_target_pairs={{0,16},{1,9},{2,18},{3,11},{4,20},{5,13},{6,22},{7,15},{8,24},{9,1... | collective-permute-start | bytes 221192 | tf_op jit(solution)/shard_map/ppermute | solution.py:35
  9.5 2.3 %collective-permute-start.7 = (bf16[32,1152]{1,0:T(8,128)(2,1)S(1)}, bf16[32,1152]{1,0:T(8,128)(2,1)S(1)}, u32[]{:S(2)}, u32[]{:S(2)}) collective-permute-start(bf16[32,1152]{1,0:T(8,128)(2,1)S(1)} %collective-permute-done.4), channel_id=1, source_target_pairs={{0,1},{1,0},{2,3},{3,2},{4,5},{5,4},{6,7},{7,6},{8,9},{9,8},{10,11... | collective-permute-start | bytes 221192 | tf_op jit(solution)/shard_map/ppermute | solution.py:35
  10.7 1.4 %collective-permute-start.6 = (bf16[32,1152]{1,0:T(8,128)(2,1)S(1)}, bf16[32,1152]{1,0:T(8,128)(2,1)S(1)}, u32[]{:S(2)}, u32[]{:S(2)}) collective-permute-start(bf16[32,1152]{1,0:T(8,128)(2,1)S(1)} %collective-permute-done.3), channel_id=1, source_target_pairs={{0,1},{1,0},{2,3},{3,2},{4,5},{5,4},{6,7},{7,6},{8,9},{9,8},{10,11... | collective-permute-start | bytes 221192 | tf_op jit(solution)/shard_map/ppermute | solution.py:35
  11.2 1.5 %collective-permute-start.5 = (bf16[32,1152]{1,0:T(8,128)(2,1)S(1)}, bf16[32,1152]{1,0:T(8,128)(2,1)S(1)}, u32[]{:S(2)}, u32[]{:S(2)}) collective-permute-start(bf16[32,1152]{1,0:T(8,128)(2,1)S(1)} %collective-permute-done.2), channel_id=1, source_target_pairs={{0,1},{1,0},{2,3},{3,2},{4,5},{5,4},{6,7},{7,6},{8,9},{9,8},{10,11... | collective-permute-start | bytes 221192 | tf_op jit(solution)/shard_map/ppermute | solution.py:35
  13.3 5.4 %collective-permute-start.10 = (f16[304,128]{1,0:T(8,128)(2,1)S(1)}, f16[304,128]{1,0:T(8,128)(2,1)S(1)}, u32[]{:S(2)}, u32[]{:S(2)}) collective-permute-start(f16[304,128]{1,0:T(8,128)(2,1)S(1)} %convert_element_type.31), channel_id=1, source_target_pairs={{0,18},{1,13},{2,16},{3,15},{4,22},{5,9},{6,20},{7,11},{8,26},{9,5... | collective-permute-start | bytes 233480 | tf_op jit(solution)/shard_map/ppermute | solution.py:35
  15.8 4.4 %collective-permute-start.9 = (f16[304,128]{1,0:T(8,128)(2,1)S(1)}, f16[304,128]{1,0:T(8,128)(2,1)S(1)}, u32[]{:S(2)}, u32[]{:S(2)}) collective-permute-start(f16[304,128]{1,0:T(8,128)(2,1)S(1)} %convert_element_type.29), channel_id=1, source_target_pairs={{0,2},{1,5},{2,0},{3,7},{4,6},{5,1},{6,4},{7,3},{8,10},{9,13},{10,... | collective-permute-start | bytes 233480 | tf_op jit(solution)/shard_map/ppermute | solution.py:35
  16.3 4.4 %collective-permute-start.8 = (f16[304,128]{1,0:T(8,128)(2,1)S(1)}, f16[304,128]{1,0:T(8,128)(2,1)S(1)}, u32[]{:S(2)}, u32[]{:S(2)}) collective-permute-start(f16[304,128]{1,0:T(8,128)(2,1)S(1)} %convert_element_type.27), channel_id=1, source_target_pairs={{0,16},{1,9},{2,18},{3,11},{4,20},{5,13},{6,22},{7,15},{8,24},{9,1... | collective-permute-start | bytes 233480 | tf_op jit(solution)/shard_map/ppermute | solution.py:35
  20.8 1.3 %collective-permute-start.11 = (f32[152,128]{1,0:T(8,128)S(1)}, f32[152,128]{1,0:T(8,128)S(1)}, u32[]{:S(2)}, u32[]{:S(2)}) collective-permute-start(f32[152,128]{1,0:T(8,128)S(1)} %get-tuple-element.17), channel_id=1, source_target_pairs={{0,1},{1,0},{2,3},{3,2},{4,5},{5,4},{6,7},{7,6},{8,9},{9,8},{10,11... | collective-permute-start | bytes 233480 | tf_op jit(solution)/shard_map/ppermute | solution.py:35
